TPU v7x, 32 devices: a whole 2x2x4 slice. The times are simulated.
32 devices in a mesh: grp: 2 (over x), comp: 8 (over z, y), lev: 2 (over core).
Axes of the slice: x: 2, y: 2, z: 4, core: 2. Of those that a mesh axis runs over, the one named last changes fastest.
Arguments:
- atm_state: float32 [4, 72, 65536], P(None, 'lev', ('grp', 'comp')), parts along dimension 2, may hold values from -6 to 6
- ocn_state: float32 [4, 80, 65536], P(None, 'lev', ('grp', 'comp')), parts along dimension 2, may hold values from -6 to 6
- atm_weights: float32 [72], P('lev'), may hold values from 0.02 to 0.2
- ocn_weights: float32 [80], P('lev'), may hold values from 0.02 to 0.2
- atm_metric: float32 [4, 32768], P(None, 'comp'), may hold values from 0.05 to 0.25
- ocn_metric: float32 [6, 32768], P(None, 'comp'), may hold values from 0.03 to 0.15
- atm_links: int32 [4, 32768], P(None, 'comp'), may hold values from 0 to 32767, as said below
- ocn_links: int32 [6, 32768], P(None, 'comp'), may hold values from 0 to 32767, as said below
- tile_weights: bfloat16 [1024, 128, 128], P(('comp', 'lev')), may hold values from -0.5 to 0.5
- tile_source: int32 [1024], P(('comp', 'lev')), may hold values from 0 to 63
- tile_target: int32 [1024], P(('comp', 'lev')), may hold values from 0 to 255, as said below
- owner_map: int32 [256], replicated, may hold values from 0 to 255, as said below
Outputs:
- atm_new: float32 [4, 72, 65536], P(None, 'lev', ('grp', 'comp')), parts along dimension 2
- ocn_new: float32 [4, 80, 65536], P(None, 'lev', ('grp', 'comp')), parts along dimension 2
- xgrid_flux: bfloat16 [512, 8, 128], P(('grp', 'comp', 'lev')), parts along dimension 0
There are 2 independent parts, one for each index of `grp`. A program takes and returns all parts, laid end to end along the dimension named above; an argument that names none is the same for every part. Nothing has to cross between parts.
Inputs may be any that keep to these rules, and one draw needn't show every extreme that they name: `atm_links`: each column's neighbour lies at most 128 columns away along the strip of 32768 columns, wrapping at its ends, and never at distance 0; distances 128 and -128 both occur. `ocn_links`: each cell's neighbour lies at most 128 cells away along the strip of 32768 cells, wrapping at its ends, and never at distance 0; distances 128 and -128 both occur. Each value once; the owner of block s is the device owner_map[s] // 16 of comp+lev. `tile_target`: of the tiles of one device at most 4 have targets of one owner, and in every draw one owner receives exactly 4 tiles from every device.
All inputs are finite; a program needn't handle non-finite values.
Results may differ from a plain program's by a relative error of at most 0.0052.
Values may be sent and summed in bfloat16 or wider, within the bound.
No kernel may reach another device: no remote copies, remote signals or barrier semaphores. Data moves between devices by JAX's collectives and lax.ppermute only.
A program may use at most 128 MiB of HBM per device.

v0:
```python
import jax
import jax.numpy as jnp
from jax import lax
from jax.sharding import PartitionSpec as P

HALO = 128
CAP = 4
XB_DEV = 16


step_size = 1.0
flux_gain = 10.0


def padded(cells, sides, width):
    for axis, dim in sides:
        count = lax.axis_size(axis)
        head = lax.slice_in_dim(cells, 0, width, axis=dim)
        tail = lax.slice_in_dim(cells, cells.shape[dim] - width, cells.shape[dim], axis=dim)
        cells = jnp.concatenate(
            [
                lax.ppermute(tail, axis, [(i, (i + 1) % count) for i in range(count)]),
                cells,
                lax.ppermute(head, axis, [((i + 1) % count, i) for i in range(count)]),
            ],
            axis=dim,
        )
    return cells


def bulk_fluxes(atm_side, ocn_side):
    temp_air = atm_side[..., 0, :]
    humid_air = atm_side[..., 1, :]
    wind_u = atm_side[..., 2, :]
    wind_v = atm_side[..., 3, :]
    temp_sea = ocn_side[..., 0, :]
    salt_sea = ocn_side[..., 1, :]
    current_u = ocn_side[..., 2, :]
    current_v = ocn_side[..., 3, :]
    shear_u = wind_u - current_u
    shear_v = wind_v - current_v
    wind_speed = jnp.sqrt(shear_u * shear_u + shear_v * shear_v + 1.0)
    stress_u = 0.8 * wind_speed * shear_u
    stress_v = 0.8 * wind_speed * shear_v
    sensible = 0.6 * wind_speed * (temp_sea - temp_air)
    saturated = 0.6 * jnp.exp(0.3 * temp_sea) * (1.0 - 0.1 * jnp.tanh(salt_sea))
    latent = 0.5 * wind_speed * (saturated - humid_air)
    atm_flux = jnp.stack([sensible, latent, -stress_u, -stress_v], axis=-2)
    ocn_flux = jnp.stack([-(sensible + latent), latent, stress_u, stress_v], axis=-2)
    return (atm_flux, ocn_flux)


def block_windows(extended, tile_size, columns):
    fields, levels = (extended.shape[0], extended.shape[1])
    blocks = columns // tile_size
    left = extended[:, :, :columns].reshape(fields, levels, blocks, tile_size)
    center = extended[:, :, HALO : HALO + columns].reshape(fields, levels, blocks, tile_size)
    right = extended[:, :, 2 * HALO : 2 * HALO + columns].reshape(fields, levels, blocks, tile_size)
    return jnp.concatenate([left, center, right], axis=3)


def diffuse(field_state, windows, metric, neighbours, first_col, all_cols, tile_size):
    fields, levels, columns = field_state.shape
    blocks = columns // tile_size
    span = tile_size + 2 * HALO
    block_start = jnp.arange(columns, dtype=jnp.int32) // tile_size * tile_size
    slots = jnp.arange(span, dtype=jnp.int32)
    operator = jnp.zeros((columns, span), jnp.float32)
    for edge in range(neighbours.shape[0]):
        position = (neighbours[edge] - first_col + HALO) % all_cols - block_start
        operator = operator + jnp.where(
            position[:, None] == slots[None, :], metric[edge][:, None], 0.0
        )
    operator = operator.reshape(blocks, tile_size, span)
    beside = jnp.einsum(
        "flbw,bcw->flbc", windows, operator, precision=lax.Precision.HIGHEST
    ).reshape(fields, levels, columns)
    total = jnp.sum(metric, axis=0)
    return beside - total[None, None, :] * field_state


def shards(
    atm_state,
    ocn_state,
    atm_weights,
    ocn_weights,
    atm_metric,
    ocn_metric,
    atm_links,
    ocn_links,
    tile_weights,
    tile_source,
    tile_target,
    owner_map,
):
    highest = lax.Precision.HIGHEST
    comp_count = lax.axis_size("comp")
    lev_count = lax.axis_size("lev")
    dev_count = comp_count * lev_count
    fields, atm_levels, columns = atm_state.shape
    tile_size = tile_weights.shape[1]
    blocks = columns // tile_size
    tiles_here = tile_weights.shape[0]
    slot_count = dev_count * CAP
    width = fields * tile_size
    part_atm = jnp.einsum("flc,l->fc", atm_state, atm_weights, precision=highest)
    part_ocn = jnp.einsum("flc,l->fc", ocn_state, ocn_weights, precision=highest)
    surf_atm, surf_ocn = lax.psum((part_atm, part_ocn), "lev")
    surface = jnp.concatenate(
        [surf_atm.reshape(fields, blocks, tile_size), surf_ocn.reshape(fields, blocks, tile_size)],
        axis=1,
    ).astype(jnp.bfloat16)
    pick_block = tile_source[:, None] == jnp.arange(2 * blocks, dtype=jnp.int32)[None, :]
    source_rows = jnp.einsum(
        "tb,fbi->fti", pick_block.astype(jnp.bfloat16), surface, preferred_element_type=jnp.float32
    ).astype(jnp.bfloat16)
    contrib = jnp.einsum(
        "fti,tij->tfj", source_rows, tile_weights, preferred_element_type=jnp.float32
    )
    xblocks = owner_map.shape[0]
    matched = tile_target[:, None] == jnp.arange(xblocks, dtype=jnp.int32)[None, :]
    placed_at = jnp.sum(jnp.where(matched, owner_map[None, :], 0), axis=1)
    owner_dev = placed_at // XB_DEV
    is_ocean = (tile_source >= blocks).astype(jnp.int32)
    segment = is_ocean * XB_DEV + placed_at % XB_DEV
    owner_hot = (owner_dev[:, None] == jnp.arange(dev_count, dtype=jnp.int32)[None, :]).astype(
        jnp.int32
    )
    lower = (
        jnp.arange(tiles_here, dtype=jnp.int32)[:, None]
        > jnp.arange(tiles_here, dtype=jnp.int32)[None, :]
    ).astype(jnp.int32)
    earlier = jnp.dot(lower, owner_hot)
    order_rank = jnp.sum(earlier * owner_hot, axis=1)
    slot_index = owner_dev * CAP + order_rank
    placing = (slot_index[:, None] == jnp.arange(slot_count, dtype=jnp.int32)[None, :]).astype(
        jnp.float32
    )
    outgoing = jnp.einsum(
        "ts,tk->sk", placing, contrib.reshape(tiles_here, width), precision=highest
    )
    labels = (
        jnp.einsum("ts,t->s", placing, (segment + 1).astype(jnp.float32), precision=highest) - 1.0
    )
    arrived, arrived_labels = (
        lax.all_to_all(outgoing, ("comp", "lev"), split_axis=0, concat_axis=0, tiled=True),
        lax.all_to_all(labels, ("comp", "lev"), split_axis=0, concat_axis=0, tiled=True),
    )
    gather_rows = (
        arrived_labels[:, None] == jnp.arange(2 * XB_DEV, dtype=jnp.float32)[None, :]
    ).astype(jnp.float32)
    sums = jnp.einsum("sb,sk->bk", gather_rows, arrived, precision=highest)
    atm_flux, ocn_flux = bulk_fluxes(
        sums[:XB_DEV].reshape(XB_DEV, fields, tile_size),
        sums[XB_DEV:].reshape(XB_DEV, fields, tile_size),
    )
    atm_flux = atm_flux.astype(jnp.bfloat16)
    ocn_flux = ocn_flux.astype(jnp.bfloat16)
    xgrid_local = jnp.concatenate([atm_flux, ocn_flux], axis=1)
    table = jnp.concatenate(
        [atm_flux.reshape(XB_DEV, width), ocn_flux.reshape(XB_DEV, width)], axis=0
    )
    answer = jnp.dot(
        gather_rows.astype(jnp.bfloat16), table, preferred_element_type=jnp.float32
    ).astype(jnp.bfloat16)
    returned = lax.all_to_all(answer, ("comp", "lev"), split_axis=0, concat_axis=0, tiled=True)
    tile_flux = jnp.dot(
        placing.astype(jnp.bfloat16), returned, preferred_element_type=jnp.float32
    ).astype(jnp.bfloat16)
    tile_flux = tile_flux.reshape(tiles_here, fields, tile_size)
    spread = jnp.einsum("tfj,tij->tfi", tile_flux, tile_weights, preferred_element_type=jnp.float32)
    per_block = jnp.einsum("tb,tfi->fbi", pick_block.astype(jnp.float32), spread, precision=highest)
    block_flux = lax.psum(per_block, "lev")
    atm_sflux = block_flux[:, :blocks].reshape(fields, columns)
    ocn_sflux = block_flux[:, blocks:].reshape(fields, columns)
    joined = jnp.concatenate([atm_state, ocn_state], axis=1)
    extended = padded(joined.astype(jnp.bfloat16), (("comp", 2),), HALO).astype(joined.dtype)
    windows = block_windows(extended, tile_size, columns)
    first_col = lax.axis_index("comp") * columns
    all_cols = columns * comp_count
    atm_new = (
        atm_state
        + step_size
        * diffuse(
            atm_state,
            windows[:, :atm_levels],
            atm_metric,
            atm_links,
            first_col,
            all_cols,
            tile_size,
        )
        + flux_gain * atm_weights[None, :, None] * atm_sflux[:, None, :]
    )
    ocn_new = (
        ocn_state
        + step_size
        * diffuse(
            ocn_state,
            windows[:, atm_levels:],
            ocn_metric,
            ocn_links,
            first_col,
            all_cols,
            tile_size,
        )
        + flux_gain * ocn_weights[None, :, None] * ocn_sflux[:, None, :]
    )
    return (atm_new, ocn_new, xgrid_local)


def solution(mesh):
    placed = (
        P(None, "lev", ("grp", "comp")),
        P(None, "lev", ("grp", "comp")),
        P("lev"),
        P("lev"),
        P(None, "comp"),
        P(None, "comp"),
        P(None, "comp"),
        P(None, "comp"),
        P(("comp", "lev"), None, None),
        P(("comp", "lev")),
        P(("comp", "lev")),
        P(),
    )
    return jax.shard_map(
        shards,
        mesh=mesh,
        in_specs=placed,
        out_specs=(
            P(None, "lev", ("grp", "comp")),
            P(None, "lev", ("grp", "comp")),
            P(("grp", "comp", "lev"), None, None),
        ),
        check_vma=False,
    )
```

profile of v0, /device:TPU:0, one launch (start us, length us, event | category | flops | bytes accessed | tf_op | source)
XLA Modules:
  0.0 206.5 jit_solution(11433859558171786173)
XLA Ops:
  7.2 2.0 convert.15
  9.3 3.4 %copy.120 = bf16[4,36,4096]{2,1,0:T(8,128)(2,1)S(1)} copy(f32[4,36,4096]{2,0,1:T(4,128)} %param.12) | data formatting | bytes 3538944 | tf_op args[0]
  12.7 0.7 pad_maximum_fusion.1
  13.4 6.0 %collective-permute-start.1 = (bf16[4,76,128]{2,1,0:T(8,128)(2,1)}, bf16[4,76,128]{2,1,0:T(8,128)(2,1)}, u32[]{:S(2)}, u32[]{:S(2)}) collective-permute-start(bf16[4,76,128]{2,1,0:T(8,128)(2,1)} %get-tuple-element.23), channel_id=1, source_target_pairs={{2,0},{4,2},{6,4},{8,6},{10,8},{12,10},{14,12},{0,14},{3,1},{5,3},... | collective-permute-start | bytes 233480 | tf_op jit(solution)/shard_map/ppermute | solution.py:24
  20.5 0.7 all_to_all.20
  21.2 6.1 %all-to-all-start = ((f32[16,4,1]{1,2,0:T(1,128)}), f32[16,4,1]{1,2,0:T(1,128)}, u32[]{:S(2)}, u32[]{:S(2)}) async-start(f32[16,4,1]{1,2,0:T(1,128)} %bitcast.13), calls=%async_computation | async-start | bytes 16384 | tf_op jit(solution)/shard_map/all_to_all | solution.py:147
  28.0 4.7 %fusion.46 = f32[1,4,4096]{2,0,1:T(1,128)S(1)} fusion(f32[4,36,4096]{2,0,1:T(4,128)} %param.12, f32[36]{0:T(128)S(1)} %copy-done.20), kind=kOutput, calls=%fused_computation.61 | convolution fusion | flops 7077888 | bytes 2424976 | tf_op jit(solution)/shard_map/flc,l->fc/dot_general | solution.py:106
  34.0 2.3 %subtract_add_fusion.5 = (s32[1,4096]{1,0:T(1,128)S(1)}, s32[1,4096]{1,0:T(1,128)}, s32[1,4096]{1,0:T(1,128)}, s32[1,4096]{1,0:T(1,128)}, s32[1,4096]{1,0:T(1,12...) fusion(s32[6,4096]{1,0:T(8,128)} %param.19, ...), kind=kLoop, calls=%fused_computation.176 | loop fusion | flops 81920 | bytes 327684 | tf_op jit(solution)/shard_map/add | solution.py:70
  38.7 3.2 %fusion.109 = f32[1,4,4096]{2,0,1:T(1,128)S(1)} fusion(f32[4,40,4096]{2,1,0:T(8,128)} %param.13, f32[40]{0:T(128)} %param.15), kind=kOutput, calls=%fused_computation.209 | convolution fusion | flops 7864320 | bytes 2687136 | tf_op jit(solution)/shard_map/flc,l->fc/dot_general | solution.py:107
  41.9 0.7 copy_bitcast_fusion.2
  42.6 4.7 %all-reduce.5 = (bf16[4,4096]{1,0:T(4,128)(2,1)S(1)}, bf16[4,4096]{1,0:T(4,128)(2,1)S(1)}) all-reduce(f32[4,4096]{1,0:T(4,128)} %get-tuple-element.65, f32[4,4096]{1,0:T(4,128)} %get-tuple-element.66), channel_id=1, replica_groups=mesh['grp'=2,'comp'=8,'lev'=2] {'lev'}, use_global_device_ids=true, to_apply=%region_4.5 | all-reduce | flops 32768 | bytes 196608 | tf_op jit(solution)/shard_map/psum | solution.py:108
  47.4 0.9 fusion.53
  48.9 0.7 reshape.539
  49.6 1.6 fusion.129
  51.2 0.7 fusion.97
  52.0 0.7 fusion.95
  52.7 0.7 fusion.93
  53.5 0.7 fusion.91
  54.2 0.7 fusion.89
  55.0 1.2 fusion.75
  56.1 8.7 %fusion.154 = f32[32,128,384]{2,1,0:T(8,128)} fusion(f32[32,128]{1,0:T(8,128)S(1)} %bitcast.143, s32[32,128]{1,0:T(8,128)S(1)} %fusion.97, f32[32,128]{1,0:T(8,128)S(1)} %bitcast.139, s32[32,128]{1,0:T(8,128)S(1)} %fusion.95, f32[32,128]{1,0:T(8,128)S(1)} %bitcast.140, s32[32,128]{1,0:T(8,128)S(1)} %fusion.93, f32[32,128]{1,0:T(8,128)S(1)} %bitcast.141, ...), kind=kLoop, calls=%fused_computation.4.clone.1 | loop fusion | flops 26738688 | bytes 6488064
  65.5 1.5 reduce_sum.36
  66.9 0.9 reduce_sum.39
  67.9 0.7 copy.67
  68.6 5.8 %all-to-all-start.1 = ((f32[16,4,512]{2,1,0:T(4,128)}), f32[16,4,512]{2,1,0:T(4,128)S(1)}, u32[]{:S(2)}, u32[]{:S(2)}) async-start(f32[16,4,512]{2,1,0:T(4,128)} %copy.67), calls=%async_computation.1 | async-start | bytes 262144 | tf_op jit(solution)/shard_map/all_to_all | solution.py:146
  74.9 1.9 reduce.3
  76.8 1.3 eq.246
  78.1 3.8 %maximum_convert_fusion = f32[4,76,4352]{2,1,0:T(8,128)} fusion(bf16[4,76,128]{2,1,0:T(8,128)(2,1)} %collective-permute-done.1, bf16[4,40,4096]{2,1,0:T(8,128)(2,1)} %copy-done.3, bf16[4,36,4096]{2,1,0:T(8,128)(2,1)S(1)} %copy.120, bf16[4,76,128]{2,1,0:T(8,128)(2,1)} %collective-permute-done), kind=kLoop, calls=%fused_computation.57 | loop fusion | flops 10584064 | bytes 7938048 | tf_op jit(solution)/shard_map/convert_element_type | solution.py:177
  81.8 11.6 %fusion.128 = (f32[4,76,4096]{2,1,0:T(8,128)}, f32[4,76,4096]{2,1,0:T(8,128)}, f32[4,76,4096]{2,1,0:T(8,128)}) fusion(f32[4,76,4352]{2,1,0:T(8,128)} %maximum_convert_fusion), kind=kLoop, calls=%fused_computation.231 | loop fusion | bytes 29884416 | tf_op jit(solution)/shard_map/slice | solution.py:58
  93.5 5.5 %reshape.520 = f32[4,76,32,128]{3,2,1,0:T(8,128)} reshape(f32[4,76,4096]{2,1,0:T(8,128)} %get-tuple-element.21) | data formatting | bytes 9961472 | tf_op jit(solution)/shard_map/reshape | solution.py:56
  98.9 7.8 %copy_dynamic-update-slice_fusion.2 = f32[4,76,32,384]{3,1,0,2:T(8,128)} fusion(f32[4,76,32,128]{3,2,1,0:T(8,128)} %reshape.520), kind=kLoop, calls=%fused_computation.34 | loop fusion | bytes 10223616
  106.8 5.5 %reshape.521 = f32[4,76,32,128]{3,2,1,0:T(8,128)} reshape(f32[4,76,4096]{2,1,0:T(8,128)} %get-tuple-element.20) | data formatting | bytes 9961472 | tf_op jit(solution)/shard_map/reshape | solution.py:57
  112.3 5.4 %reshape.522 = f32[4,76,32,128]{3,2,1,0:T(8,128)} reshape(f32[4,76,4096]{2,1,0:T(8,128)} %get-tuple-element.19) | data formatting | bytes 9961472 | tf_op jit(solution)/shard_map/reshape | solution.py:58
  117.7 7.9 %copy_dynamic-update-slice_fusion.1 = f32[4,76,32,384]{3,1,0,2:T(8,128)} fusion(f32[4,76,32,384]{3,1,0,2:T(8,128)} %copy_dynamic-update-slice_fusion.2, f32[4,76,32,128]{3,2,1,0:T(8,128)} %reshape.521), kind=kLoop, calls=%fused_computation.33 | loop fusion | bytes 10223616
  125.5 5.5 %copy_dynamic-update-slice_fusion = f32[4,76,32,384]{3,1,0,2:T(8,128)} fusion(f32[4,76,32,384]{3,1,0,2:T(8,128)} %copy_dynamic-update-slice_fusion.1, f32[4,76,32,128]{3,2,1,0:T(8,128)S(1)} %copy-done.2), kind=kLoop, calls=%fused_computation.32 | loop fusion | bytes 10223616 | tf_op jit(solution)/shard_map/concatenate | solution.py:59
  131.1 7.0 %fusion.156 = f32[4,36,32,384]{3,1,0,2:T(8,128)} fusion(f32[4,76,32,384]{3,1,0,2:T(8,128)} %copy_dynamic-update-slice_fusion), kind=kLoop, calls=%fused_computation.1.clone.clone.clone.2 | loop fusion | bytes 14155776 | tf_op jit(solution)/shard_map/flbw,bcw->flbc/dot_general | solution.py:75
  138.9 0.7 all_to_all.24
  139.5 6.0 %all-to-all-start.2 = ((bf16[16,4,512]{2,1,0:T(4,128)(2,1)}), bf16[16,4,512]{2,1,0:T(4,128)(2,1)S(1)}, u32[]{:S(2)}, u32[]{:S(2)}) async-start(bf16[16,4,512]{2,1,0:T(4,128)(2,1)} %all_to_all.24), calls=%async_computation.2 | async-start | bytes 131072 | tf_op jit(solution)/shard_map/all_to_all | solution.py:166
  145.7 15.0 %fusion.48 = f32[4,36,32,128]{3,1,0,2:T(8,128)} fusion(f32[32,128]{1,0:T(8,128)S(1)} %bitcast.167, s32[32,128]{1,0:T(8,128)S(1)} %copy-done.8, f32[32,128]{1,0:T(8,128)S(1)} %bitcast.165, s32[32,128]{1,0:T(8,128)S(1)} %copy-done.9, f32[32,128]{1,0:T(8,128)S(1)} %bitcast.166, s32[32,128]{1,0:T(8,128)S(1)} %copy-done.10, f32[32,128]{1,0:T(8,128)S(1)} %bitcast.164, ...), kind=kOutput, calls=%fused_computation.65 | convolution fusion | flops 2735210496 | bytes 9568256 | tf_op jit(solution)/shard_map/flbw,bcw->flbc/dot_general | solution.py:75
  160.7 7.9 %slice.171 = f32[4,40,32,384]{3,1,0,2:T(8,128)} slice(f32[4,76,32,384]{3,1,0,2:T(8,128)} %copy_dynamic-update-slice_fusion), slice={[0:4], [36:76], [0:32], [0:384]} | slice | bytes 15728640 | tf_op jit(solution)/shard_map/slice | solution.py:200
  168.8 1.2 fusion.134
  170.0 0.9 convolution_bitcast_fusion
  170.9 12.9 %fusion.3 = f32[32,128,160]{1,2,0} fusion(f32[32,384,160]{1,2,0:T(8,128)} %bitcast.130, f32[32,128,384]{2,1,0:T(8,128)} %fusion.154), kind=kOutput, calls=%fused_computation.3 | convolution fusion | flops 3019898880 | bytes 16777216
  183.8 2.8 %copy.63 = f32[4,36,32,128]{3,2,0,1:T(8,128)} copy(f32[4,36,32,128]{3,1,0,2:T(8,128)S(1)} %copy-done.5) | data formatting | bytes 4718592 | tf_op jit(solution)/shard_map/flbw,bcw->flbc/transpose | solution.py:75
  186.6 3.5 %reshape.523 = f32[4,36,4096]{2,0,1:T(4,128)} reshape(f32[4,36,32,128]{3,2,0,1:T(8,128)} %copy.63) | data formatting | bytes 4718592 | tf_op jit(solution)/shard_map/reshape | solution.py:77
  190.8 1.0 slice_bitcast_fusion
  192.0 5.7 %multiply_add_fusion = f32[4,36,4096]{2,0,1:T(4,128)} fusion(f32[4,36,4096]{2,0,1:T(4,128)} %param.12, f32[4,36,4096]{2,0,1:T(4,128)} %reshape.523, f32[4,4096]{1,0:T(4,128)S(1)} %bitcast.133, f32[36]{0:T(128)S(1)} %copy-done.24, f32[4096]{0:T(1024)S(1)} %copy-done.7), kind=kLoop, calls=%fused_computation.64 | loop fusion | flops 2949120 | bytes 7159952 | tf_op jit(solution)/shard_map/add | solution.py:182
  197.6 2.0 fusion.45
  (101 shorter events, 9.0 us)
Async XLA Ops:
  7.2 41.1 %copy-start = (bf16[64,128,128]{2,1,0:T(8,128)(2,1)S(1)}, bf16[64,128,128]{2,1,0:T(8,128)(2,1)}, u32[]{:S(2)}) copy-start(bf16[64,128,128]{2,1,0:T(8,128)(2,1)} %param.20) | copy-start | bytes 6291460
  7.2 12.3 %copy-start.19 = (s32[256]{0:T(256)S(1)}, s32[256]{0:T(256)}, u32[]{:S(2)}) copy-start(s32[256]{0:T(256)} %param.23) | copy-start | bytes 3076
  7.2 12.3 %copy-start.26 = (s32[64]{0:T(128)S(1)}, s32[64]{0:T(128)}, u32[]{:S(2)}) copy-start(s32[64]{0:T(128)} %param.22) | copy-start | bytes 772
  7.2 13.1 %copy-start.22 = (s32[64]{0:T(128)S(1)}, s32[64]{0:T(128)}, u32[]{:S(2)}) copy-start(s32[64]{0:T(128)} %param.21) | copy-start | bytes 772
  7.2 20.8 %copy-start.20 = (f32[36]{0:T(128)S(1)}, f32[36]{0:T(128)}, u32[]{:S(2)}) copy-start(f32[36]{0:T(128)} %param.14) | copy-start | bytes 436
  9.3 3.5 %copy-start.3 = (bf16[4,40,4096]{2,1,0:T(8,128)(2,1)}, bf16[4,40,4096]{2,1,0:T(8,128)(2,1)S(1)}, u32[]{:S(2)}) copy-start(bf16[4,40,4096]{2,1,0:T(8,128)(2,1)S(1)} %convert.15) | copy-start | bytes 3932164
  9.3 24.0 %copy-start.6 = (f32[4,4096]{1,0:T(4,128)S(1)}, f32[4,4096]{1,0:T(4,128)}, u32[]{:S(2)}) copy-start(f32[4,4096]{1,0:T(4,128)} %param.16) | copy-start | bytes 196612
  13.4 64.6 %collective-permute-start.1 = (bf16[4,76,128]{2,1,0:T(8,128)(2,1)}, bf16[4,76,128]{2,1,0:T(8,128)(2,1)}, u32[]{:S(2)}, u32[]{:S(2)}) collective-permute-start(bf16[4,76,128]{2,1,0:T(8,128)(2,1)} %get-tuple-element.23), channel_id=1, source_target_pairs={{2,0},{4,2},{6,4},{8,6},{10,8},{12,10},{14,12},{0,14},{3,1},{5,3},... | collective-permute-start | bytes 233480 | tf_op jit(solution)/shard_map/ppermute | solution.py:24
  19.4 58.6 %collective-permute-start = (bf16[4,76,128]{2,1,0:T(8,128)(2,1)}, bf16[4,76,128]{2,1,0:T(8,128)(2,1)}, u32[]{:S(2)}, u32[]{:S(2)}) collective-permute-start(bf16[4,76,128]{2,1,0:T(8,128)(2,1)} %get-tuple-element.22), channel_id=1, source_target_pairs={{0,2},{2,4},{4,6},{6,8},{8,10},{10,12},{12,14},{14,0},{1,3},{3,5},... | collective-permute-start | bytes 233480 | tf_op jit(solution)/shard_map/ppermute | solution.py:22
  19.8 0.5 copy-start.17
  21.2 47.4 %all-to-all-start = ((f32[16,4,1]{1,2,0:T(1,128)}), f32[16,4,1]{1,2,0:T(1,128)}, u32[]{:S(2)}, u32[]{:S(2)}) async-start(f32[16,4,1]{1,2,0:T(1,128)} %bitcast.13), calls=%async_computation | async-start | bytes 16384 | tf_op jit(solution)/shard_map/all_to_all | solution.py:147
  49.6 15.3 %copy-start.21 = (f32[40]{0:T(128)S(1)}, f32[40]{0:T(128)}, u32[]{:S(2)}) copy-start(f32[40]{0:T(128)} %param.15) | copy-start | bytes 484
  68.6 69.5 %all-to-all-start.1 = ((f32[16,4,512]{2,1,0:T(4,128)}), f32[16,4,512]{2,1,0:T(4,128)S(1)}, u32[]{:S(2)}, u32[]{:S(2)}) async-start(f32[16,4,512]{2,1,0:T(4,128)} %copy.67), calls=%async_computation.1 | async-start | bytes 262144 | tf_op jit(solution)/shard_map/all_to_all | solution.py:146
  117.7 7.9 %copy-start.2 = (f32[4,76,32,128]{3,2,1,0:T(8,128)S(1)}, f32[4,76,32,128]{3,2,1,0:T(8,128)}, u32[]{:S(2)}) copy-start(f32[4,76,32,128]{3,2,1,0:T(8,128)} %reshape.522) | copy-start | bytes 14942212
  131.0 7.1 %copy-start.16 = (f32[64]{0:T(128)S(1)}, f32[64]{0:T(128)}, u32[]{:S(2)}) copy-start(f32[64]{0:T(128)} %eq.246) | copy-start | bytes 772
  131.0 14.6 %copy-start.8 = (s32[32,128]{1,0:T(8,128)S(1)}, s32[32,128]{1,0:T(8,128)}, u32[]{:S(2)}) copy-start(s32[32,128]{1,0:T(8,128)} %fusion.85) | copy-start | bytes 49156
  131.0 14.6 %copy-start.9 = (s32[32,128]{1,0:T(8,128)S(1)}, s32[32,128]{1,0:T(8,128)}, u32[]{:S(2)}) copy-start(s32[32,128]{1,0:T(8,128)} %fusion.83) | copy-start | bytes 49156
  131.0 14.6 %copy-start.10 = (s32[32,128]{1,0:T(8,128)S(1)}, s32[32,128]{1,0:T(8,128)}, u32[]{:S(2)}) copy-start(s32[32,128]{1,0:T(8,128)} %fusion.81) | copy-start | bytes 49156
  131.0 14.6 %copy-start.11 = (s32[32,128]{1,0:T(8,128)S(1)}, s32[32,128]{1,0:T(8,128)}, u32[]{:S(2)}) copy-start(s32[32,128]{1,0:T(8,128)} %fusion.78) | copy-start | bytes 49156
  131.0 14.6 %copy-start.12 = (f32[1,4096]{1,0:T(1,128)S(1)}, f32[1,4096]{1,0:T(1,128)}, u32[]{:S(2)}) copy-start(f32[1,4096]{1,0:T(1,128)} %get-tuple-element.44) | copy-start | bytes 49156
  131.0 14.6 %copy-start.13 = (f32[1,4096]{1,0:T(1,128)S(1)}, f32[1,4096]{1,0:T(1,128)}, u32[]{:S(2)}) copy-start(f32[1,4096]{1,0:T(1,128)} %get-tuple-element.45) | copy-start | bytes 49156
  131.1 14.6 %copy-start.14 = (f32[1,4096]{1,0:T(1,128)S(1)}, f32[1,4096]{1,0:T(1,128)}, u32[]{:S(2)}) copy-start(f32[1,4096]{1,0:T(1,128)} %get-tuple-element.46) | copy-start | bytes 49156
  131.1 14.6 %copy-start.15 = (f32[1,4096]{1,0:T(1,128)S(1)}, f32[1,4096]{1,0:T(1,128)}, u32[]{:S(2)}) copy-start(f32[1,4096]{1,0:T(1,128)} %get-tuple-element.47) | copy-start | bytes 49156
  139.5 29.0 %all-to-all-start.2 = ((bf16[16,4,512]{2,1,0:T(4,128)(2,1)}), bf16[16,4,512]{2,1,0:T(4,128)(2,1)S(1)}, u32[]{:S(2)}, u32[]{:S(2)}) async-start(bf16[16,4,512]{2,1,0:T(4,128)(2,1)} %all_to_all.24), calls=%async_computation.2 | async-start | bytes 131072 | tf_op jit(solution)/shard_map/all_to_all | solution.py:166
  145.5 45.2 %all-reduce.4.cloned.1.call-start = ((), (), s32[]{:S(2)}) async-start(), calls=%async_computation.3 | async-start | bytes 262144 | tf_op jit(solution)/shard_map/psum | solution.py:173
  160.7 7.9 %copy-start.18 = (s32[64]{0:T(128)S(1)}, s32[64]{0:T(128)}, u32[]{:S(2)}) copy-start(s32[64]{0:T(128)} %copy-done.17) | copy-start | bytes 772
  160.7 9.4 %copy-start.23 = (s32[64]{0:T(128)S(1)}, s32[64]{0:T(128)}, u32[]{:S(2)}) copy-start(s32[64]{0:T(128)} %param.21) | copy-start | bytes 772
  170.9 12.9 %copy-start.5 = (f32[4,36,32,128]{3,1,0,2:T(8,128)S(1)}, f32[4,36,32,128]{3,1,0,2:T(8,128)}, u32[]{:S(2)}) copy-start(f32[4,36,32,128]{3,1,0,2:T(8,128)} %fusion.48) | copy-start | bytes 7077892
  183.8 8.1 %copy-start.7 = (f32[4096]{0:T(1024)S(1)}, f32[4096]{0:T(1024)}, u32[]{:S(2)}) copy-start(f32[4096]{0:T(1024)} %reduce_sum.36) | copy-start | bytes 49156
  183.8 8.1 %copy-start.24 = (f32[36]{0:T(128)S(1)}, f32[36]{0:T(128)}, u32[]{:S(2)}) copy-start(f32[36]{0:T(128)} %broadcast_multiply_fusion.1) | copy-start | bytes 436
  186.6 11.0 %copy-start.25 = (f32[40]{0:T(128)S(1)}, f32[40]{0:T(128)}, u32[]{:S(2)}) copy-start(f32[40]{0:T(128)} %broadcast_multiply_fusion) | copy-start | bytes 484
  190.8 6.9 %copy-start.1 = (f32[4,40,4096]{2,1,0:T(8,128)S(1)}, f32[4,40,4096]{2,1,0:T(8,128)}, u32[]{:S(2)}) copy-start(f32[4,40,4096]{2,1,0:T(8,128)} %param.13) | copy-start | bytes 7864324
  190.8 6.9 %copy-start.4 = (f32[32,128,160]{1,2,0:S(1)}, f32[32,128,160]{1,2,0}, u32[]{:S(2)}) copy-start(f32[32,128,160]{1,2,0} %fusion.3) | copy-start | bytes 7864324
Sparse Core Ops, SparseCore 0:
  171.0 19.2 all-reduce.3
where the time goes:
time: 208 us; the launch traced here: 206 us
  local copies, waits for them, and re-layouts  84 us (40%)
  matrix products  41.5 us (20%)
  other arithmetic  37.7 us (18%)
  starting transfers between devices  24 us (12%)
  between operations  14.5 us (7%)
  blocking collectives  4.73 us (2%)
    unnamed x63, local copies, waits for them, and re-layouts  21.5 us
    dot_general x1, matrix products, diffuse(): jnp.einsum('flbw,bcw->flbc', windows, operator, precision=lax.Precision.H...  15 us
    unnamed x1, matrix products  12.9 us
    slice x1, local copies, waits for them, and re-layouts, block_windows(): extended[:, :, 2 * HALO:2 * HALO + columns]  11.6 us
    unnamed x1, other arithmetic  8.74 us
    slice x1, local copies, waits for them, and re-layouts, shards(): windows[:, atm_levels:]  7.91 us
    dot_general x1, local copies, waits for them, and re-layouts, diffuse(): jnp.einsum('flbw,bcw->flbc', windows, operator, precision=lax.Precision.H...  7.02 us
    sub x10, other arithmetic, diffuse(): position = (neighbours[edge] - first_col + HALO) % all_cols - block_start  6.17 us
  transfers between devices with their start and end apart: 6, of which 0 were waited for; matrix products, arithmetic and copies ran while one was open for 69% of the time, Pallas kernels for 0%

commit v1 on v0

v1 whole, which is shorter than its diff:
```python
import functools

import jax
import jax.numpy as jnp
from jax import lax
from jax.experimental import pallas as pl
from jax.experimental.pallas import tpu as pltpu
from jax.sharding import PartitionSpec as P

HALO = 128
CAP = 4
XB_DEV = 16
TILE = 128
step_size = 1.0
flux_gain = 10.0
BF16 = jnp.bfloat16
F32 = jnp.float32
BOTH = ("comp", "lev")


def in_vmem():
    return pl.BlockSpec(memory_space=pltpu.VMEM)


def in_smem():
    return pl.BlockSpec(memory_space=pltpu.SMEM)


def in_hbm():
    return pl.BlockSpec(memory_space=pl.ANY)


def held(array):
    return pltpu.with_memory_space_constraint(array, pltpu.VMEM)


def outside(array):
    return pltpu.with_memory_space_constraint(array, pltpu.HBM)


def limit(mib):
    return pltpu.CompilerParams(vmem_limit_bytes=mib * 1024 * 1024)


def to_rows(state):
    fields, levels, columns = state.shape
    blocks = columns // TILE
    split = state.transpose(1, 0, 2).reshape(levels, fields, blocks, TILE)
    return split.transpose(0, 2, 1, 3).reshape(levels, blocks * fields, TILE)


def from_rows(rows, fields):
    levels, count, _ = rows.shape
    blocks = count // fields
    split = rows.reshape(levels, blocks, fields, TILE).transpose(0, 2, 1, 3)
    return split.reshape(levels, fields, blocks * TILE).transpose(1, 0, 2)


def surface_kernel(
    chunks, atm_hbm, ocn_hbm, atm_w, ocn_w, part_ref, head_ref, tail_ref, atm_wide, ocn_wide, atm_ref, ocn_ref,
    atm_s, ocn_s, sems, few_sems,
):
    levels, atm_rows, _ = atm_ref.shape
    fields, ocn_levels, columns = ocn_ref.shape
    deep = atm_rows // chunks
    wide = columns // chunks
    copies = []
    for chunk in range(chunks):
        rows = pl.ds(chunk * deep, deep)
        cols = pl.ds(chunk * wide, wide)
        for which, (src, dst) in enumerate(
            ((atm_hbm.at[:, rows, :], atm_ref.at[:, rows, :]), (ocn_hbm.at[:, :, cols], ocn_ref.at[:, :, cols]))
        ):
            copy = pltpu.make_async_copy(src, dst, sems.at[chunk, which])
            copy.start()
            copies.append(copy)
    few = [
        pltpu.make_async_copy(atm_w, atm_s, few_sems.at[0]),
        pltpu.make_async_copy(ocn_w, ocn_s, few_sems.at[1]),
    ]
    for copy in few:
        copy.start()
    for copy in few:
        copy.wait()
    for level in range(levels):
        atm_wide[level] = jnp.full((8, TILE), atm_s[level], F32)
    for level in range(ocn_levels):
        ocn_wide[level : level + 1] = jnp.full((1, TILE), ocn_s[level], F32)
    for chunk in range(chunks):
        copies[2 * chunk].wait()
        copies[2 * chunk + 1].wait()

        def one_pair(pair, carry):
            rows = pl.ds(pl.multiple_of(pair * 8, 8), 8)
            atm = atm_ref[0, rows, :] * atm_wide[0]
            for level in range(1, levels):
                atm = atm + atm_ref[level, rows, :] * atm_wide[level]
            for half in range(2):
                block = 2 * pair + half
                cols = pl.ds(pl.multiple_of(block * TILE, TILE), TILE)
                ocn = [
                    jnp.sum(ocn_ref[field, :, cols] * ocn_wide[...], axis=0, keepdims=True) for field in range(fields)
                ]
                part_ref[block] = jnp.concatenate([atm[half * fields : (half + 1) * fields]] + ocn, axis=0)
            return carry

        lax.fori_loop(chunk * (deep // 8), (chunk + 1) * (deep // 8), one_pair, 0)
    for ref, row, col in ((head_ref, 0, 0), (tail_ref, atm_rows - fields, columns - HALO)):
        stack = [atm_ref[level, row : row + fields, :] for level in range(levels)]
        stack += [ocn_ref[field, :, col : col + HALO] for field in range(fields)]
        ref[...] = jnp.concatenate(stack, axis=0).astype(BF16)


def surface(atm_rows, ocn_state, atm_weights, ocn_weights):
    levels, count, _ = atm_rows.shape
    fields, ocn_levels, columns = ocn_state.shape
    rows = fields * (levels + ocn_levels)
    chunks = 4
    return pl.pallas_call(
        functools.partial(surface_kernel, chunks),
        out_shape=(
            jax.ShapeDtypeStruct((columns // TILE, 2 * fields, TILE), F32),
            jax.ShapeDtypeStruct((rows, HALO), BF16),
            jax.ShapeDtypeStruct((rows, HALO), BF16),
            jax.ShapeDtypeStruct((levels, 8, TILE), F32),
            jax.ShapeDtypeStruct((ocn_levels, TILE), F32),
        ),
        in_specs=[in_hbm()] * 4,
        out_specs=(in_vmem(),) * 5,
        scratch_shapes=[
            pltpu.VMEM(atm_rows.shape, F32),
            pltpu.VMEM(ocn_state.shape, F32),
            pltpu.SMEM((levels,), F32),
            pltpu.SMEM((ocn_levels,), F32),
            pltpu.SemaphoreType.DMA((chunks, 2)),
            pltpu.SemaphoreType.DMA((2,)),
        ],
        compiler_params=limit(12),
        name="surface",
    )(outside(atm_rows), outside(ocn_state), outside(atm_weights), outside(ocn_weights))


def contrib_kernel(blocks, source_ref, own_ref, other_ref, weight_ref, select_ref, label_ref, out_ref, surf_ref, row_ref):
    surf_ref[...] = (own_ref[...] + other_ref[...]).astype(BF16).astype(F32)
    tiles = weight_ref.shape[0]
    both = own_ref.shape[1]
    devs, depth, _ = out_ref.shape

    def one_tile(tile, carry):
        block = lax.rem(source_ref[tile], blocks)
        row_ref[pl.ds(pl.multiple_of(both * tile, both), both)] = jnp.dot(
            surf_ref[block].astype(BF16), weight_ref[tile], preferred_element_type=F32
        )
        return carry

    lax.fori_loop(0, tiles, one_tile, 0, unroll=True)
    placed = jnp.dot(select_ref[...], row_ref[...].astype(BF16), preferred_element_type=F32)
    placed = placed.reshape(devs, depth - 8, TILE)
    out_ref[...] = jnp.concatenate([placed, label_ref[...]], axis=1).astype(BF16)


def contributions(own, other, tile_source, tile_weights, select, labels):
    blocks, both, _ = own.shape
    tiles = tile_weights.shape[0]
    devs = labels.shape[0]
    return pl.pallas_call(
        functools.partial(contrib_kernel, blocks),
        out_shape=jax.ShapeDtypeStruct((devs, CAP * both // 2 + 8, TILE), BF16),
        in_specs=[in_smem()] + [in_vmem()] * 5,
        out_specs=in_vmem(),
        scratch_shapes=[pltpu.VMEM(own.shape, F32), pltpu.VMEM((tiles * both, TILE), F32)],
        compiler_params=limit(8),
        name="contributions",
    )(tile_source, own, other, tile_weights, select, labels)


def bulk_fluxes(air, sea):
    shear_u = air[2] - sea[2]
    shear_v = air[3] - sea[3]
    wind_speed = jnp.sqrt(shear_u * shear_u + shear_v * shear_v + 1.0)
    stress_u = 0.8 * wind_speed * shear_u
    stress_v = 0.8 * wind_speed * shear_v
    sensible = 0.6 * wind_speed * (sea[0] - air[0])
    saturated = 0.6 * jnp.exp(0.3 * sea[0]) * (1.0 - 0.1 * jnp.tanh(sea[1]))
    latent = 0.5 * wind_speed * (saturated - air[1])
    return (
        [sensible, latent, -stress_u, -stress_v],
        [-(sensible + latent), latent, stress_u, stress_v],
    )


def flux_kernel(fields, arrived_ref, grid_ref, answer_ref):
    devs, depth, _ = arrived_ref.shape
    per = fields * CAP
    arrived = arrived_ref[...].astype(F32)
    values = arrived[:, :per].reshape(devs * per, TILE).astype(BF16)
    labels = jnp.concatenate([arrived[:, per:]] * (per // 8), axis=1)
    field = lax.broadcasted_iota(jnp.int32, labels.shape, 1) // CAP
    codes = (labels + (field * (2 * XB_DEV)).astype(F32)).reshape(devs * per, TILE)
    codes = jnp.where(labels.reshape(devs * per, TILE) < 0.0, -1.0, codes)
    lane = lax.broadcasted_iota(jnp.int32, (1, TILE), 1)
    side, rest = lane // (fields * XB_DEV), lane % (fields * XB_DEV)
    code_of = side * XB_DEV + rest % XB_DEV + rest // XB_DEV * (2 * XB_DEV)
    hot = jnp.where(codes == code_of.astype(F32), 1.0, 0.0).astype(BF16)
    sums = lax.dot_general(hot, values, (((0,), (0,)), ((), ())), preferred_element_type=F32)
    rows = [sums[XB_DEV * k : XB_DEV * (k + 1)] for k in range(2 * fields)]
    atm_flux, ocn_flux = bulk_fluxes(rows[:fields], rows[fields:])
    table = jnp.concatenate(atm_flux + ocn_flux, axis=0).astype(BF16)
    to = lax.broadcasted_iota(jnp.int32, (TILE, TILE), 0)
    at = lax.broadcasted_iota(jnp.int32, (TILE, TILE), 1)
    both = 2 * fields
    moves = jnp.where(at == to % both * XB_DEV + to // both, 1.0, 0.0).astype(BF16)
    moved = jnp.dot(moves, table, preferred_element_type=F32)
    grid_ref[...] = moved.reshape(XB_DEV, both, TILE).astype(BF16)
    answer = jnp.dot(hot, table, preferred_element_type=F32)
    answer_ref[...] = answer.reshape(devs, per, TILE).astype(BF16)


def fluxes(arrived, fields):
    devs, _, _ = arrived.shape
    return pl.pallas_call(
        functools.partial(flux_kernel, fields),
        out_shape=(
            jax.ShapeDtypeStruct((XB_DEV, 2 * fields, TILE), BF16),
            jax.ShapeDtypeStruct((devs, fields * CAP, TILE), BF16),
        ),
        in_specs=[in_vmem()],
        out_specs=(in_vmem(),) * 2,
        compiler_params=limit(8),
        name="fluxes",
    )(arrived)


def merged(places, values):
    sums = []
    for k, value in enumerate(values):
        whole = value
        for j in range(k):
            whole = whole + jnp.where(places[j] == places[k], values[j], 0.0)
        sums.append(whole)
    return sums


def fill_operator(out, links, metric, cols, first_col, all_cols):
    edges = links.shape[0]
    lane = lax.broadcasted_iota(jnp.int32, (edges, TILE), 1)
    away = links[:, cols] - (first_col + lane)
    away = jnp.where(away > all_cols // 2, away - all_cols, away)
    away = jnp.where(away < -(all_cols // 2), away + all_cols, away)
    place = (away + lane).astype(F32)
    value = metric[:, cols]
    places = [jnp.broadcast_to(place[k : k + 1], (8, TILE)) for k in range(edges)]
    values = [jnp.broadcast_to(value[k : k + 1], (8, TILE)) for k in range(edges)]
    sums = merged(places, values)
    places = [jnp.concatenate([v, v], axis=0).astype(BF16) for v in places]
    sums = [jnp.concatenate([v, v], axis=0).astype(BF16) for v in sums]
    row = lax.broadcasted_iota(jnp.int32, (16, TILE), 0).astype(F32)
    for group in range((TILE + 2 * HALO) // 16):
        here = (row + float(16 * group - HALO)).astype(BF16)
        found = jnp.zeros((16, TILE), BF16)
        for k in range(edges):
            found = jnp.where(places[k] == here, sums[k], found)
        out[16 * group : 16 * (group + 1)] = found
    return 1.0 - step_size * jnp.sum(value, axis=0, keepdims=True)


def diffuse_kernel(
    all_cols, start_ref, atm_hbm, ocn_hbm, atm_links, ocn_links, atm_metric, ocn_metric, atm_out, ocn_out, ends_ref,
    atm_ref, ocn_ref, even_ref, odd_ref, wide_ref, op_ref, atm_new, ocn_new, in_sems, out_sems,
):
    levels, padded_rows, _ = atm_ref.shape
    fields, ocn_levels, columns = ocn_ref.shape
    pairs = columns // (2 * TILE)
    span = TILE + 2 * HALO

    def into(pair):
        rows = pl.ds(pl.multiple_of(8 * pair, 8), 8)
        lands = pl.ds(pl.multiple_of(8 * pair + 8, 8), 8)
        cols = pl.ds(pl.multiple_of(2 * TILE * pair, TILE), 2 * TILE)
        return [
            pltpu.make_async_copy(atm_hbm.at[:, rows, :], atm_ref.at[:, lands, :], in_sems.at[pair, 0]),
            pltpu.make_async_copy(ocn_hbm.at[:, :, cols], ocn_ref.at[:, :, cols], in_sems.at[pair, 1]),
        ]

    def out_of(pair):
        slot = lax.rem(pair, 2)
        rows = pl.ds(pl.multiple_of(8 * pair, 8), 8)
        cols = pl.ds(pl.multiple_of(2 * TILE * pair, TILE), 2 * TILE)
        return [
            pltpu.make_async_copy(atm_new.at[slot], atm_out.at[:, rows, :], out_sems.at[slot, 0]),
            pltpu.make_async_copy(ocn_new.at[slot], ocn_out.at[:, :, cols], out_sems.at[slot, 1]),
        ]

    for pair in range(pairs):
        for copy in into(pair):
            copy.start()
    atm_ref[:, :8, :] = jnp.zeros((levels, 8, TILE), F32)
    atm_ref[:, padded_rows - 8 :, :] = jnp.zeros((levels, 8, TILE), F32)
    wide_ref[:, :HALO] = jnp.zeros((fields * ocn_levels, HALO), BF16)
    wide_ref[:, HALO + columns :] = jnp.zeros((fields * ocn_levels, HALO), BF16)

    def narrow(pair):
        both = atm_ref[:, pl.ds(pl.multiple_of(8 * pair, 8), 16), :]
        odd_ref[pair] = both[:, 4:12].reshape(levels * 8, TILE).astype(BF16)
        even_ref[pair] = both[:, 8:].reshape(levels * 8, TILE).astype(BF16)
        cols = pl.ds(pl.multiple_of(2 * TILE * pair, TILE), 2 * TILE)
        lands = pl.ds(pl.multiple_of(2 * TILE * pair + HALO, TILE), 2 * TILE)
        stack = jnp.concatenate([ocn_ref[field, :, cols] for field in range(fields)], axis=0)
        wide_ref[:, lands] = stack.astype(BF16)

    for copy in into(0):
        copy.wait()
    narrow(0)
    top = lax.broadcasted_iota(jnp.int32, (8, TILE), 0) < fields

    def one_pair(pair, carry):
        @pl.when(pair + 1 < pairs)
        def _():
            for copy in into(pair + 1):
                copy.wait()
            narrow(pair + 1)

        @pl.when(pair + 1 == pairs)
        def _():
            both = atm_ref[:, pl.ds(8 * pairs, 16), :]
            odd_ref[pairs] = both[:, 4:12].reshape(levels * 8, TILE).astype(BF16)

        @pl.when(pair >= 2)
        def _():
            for copy in out_of(pair - 2):
                copy.wait()

        slot = lax.rem(pair, 2)
        keeps = []
        for half in range(2):
            block = 2 * pair + half
            first_col = start_ref[0] + block * TILE
            cols = pl.ds(pl.multiple_of(block * TILE, TILE), TILE)
            for which, (links, metric) in enumerate(((atm_links, atm_metric), (ocn_links, ocn_metric))):
                keeps.append(fill_operator(op_ref.at[which, half], links, metric, cols, first_col, all_cols))
        beside = jnp.dot(
            jnp.concatenate([odd_ref[pair], even_ref[pair], odd_ref[pair + 1]], axis=1),
            jnp.concatenate([op_ref[0, 0], op_ref[0, 1]], axis=1),
            preferred_element_type=F32,
        )
        keep = jnp.where(top, keeps[0], keeps[2])
        lands = pl.ds(pl.multiple_of(8 * pair + 8, 8), 8)
        for level in range(levels):
            rows = beside[8 * level : 8 * level + 8]
            atm_new[slot, level] = atm_ref[level, lands, :] * keep + step_size * jnp.where(
                top, rows[:, :TILE], rows[:, TILE:]
            )
        for half in range(2):
            at = pl.multiple_of(2 * TILE * pair + half * TILE, TILE)
            beside = jnp.dot(wide_ref[:, pl.ds(at, span)], op_ref[1, half], preferred_element_type=F32)
            for field in range(fields):
                ocn_new[slot, field, :, half * TILE : (half + 1) * TILE] = (
                    ocn_ref[field, :, pl.ds(at, TILE)] * keeps[1 + 2 * half]
                    + step_size * beside[field * ocn_levels : (field + 1) * ocn_levels]
                )
        for copy in out_of(pair):
            copy.start()

        @pl.when(pair == 0)
        def _():
            for which in range(2):
                ends_ref[0, which] = op_ref[which, 0, :HALO]

        @pl.when(pair + 1 == pairs)
        def _():
            for which in range(2):
                ends_ref[1, which] = op_ref[which, 1, HALO + TILE :]

        return carry

    lax.fori_loop(0, pairs, one_pair, 0)
    for pair in (pairs - 2, pairs - 1):
        for copy in out_of(pair):
            copy.wait()


def diffusion(start, all_cols, atm_rows, ocn_state, atm_links, ocn_links, atm_metric, ocn_metric):
    levels, count, _ = atm_rows.shape
    fields, ocn_levels, columns = ocn_state.shape
    pairs = columns // (2 * TILE)
    span = TILE + 2 * HALO
    return pl.pallas_call(
        functools.partial(diffuse_kernel, all_cols),
        out_shape=(
            pltpu.HBM(atm_rows.shape, F32),
            pltpu.HBM(ocn_state.shape, F32),
            jax.ShapeDtypeStruct((2, 2, HALO, TILE), BF16),
        ),
        in_specs=[in_smem(), in_hbm(), in_hbm()] + [in_vmem()] * 4,
        out_specs=(in_hbm(), in_hbm(), in_vmem()),
        scratch_shapes=[
            pltpu.VMEM((levels, count + 16, TILE), F32),
            pltpu.VMEM(ocn_state.shape, F32),
            pltpu.VMEM((pairs, levels * 8, TILE), BF16),
            pltpu.VMEM((pairs + 1, levels * 8, TILE), BF16),
            pltpu.VMEM((fields * ocn_levels, columns + 2 * HALO), BF16),
            pltpu.VMEM((2, 2, span, TILE), BF16),
            pltpu.VMEM((2, levels, 8, TILE), F32),
            pltpu.VMEM((2, fields, ocn_levels, 2 * TILE), F32),
            pltpu.SemaphoreType.DMA((pairs, 2)),
            pltpu.SemaphoreType.DMA((2, 2)),
        ],
        compiler_params=limit(24),
        name="diffusion",
    )(start, outside(atm_rows), outside(ocn_state), atm_links, ocn_links, atm_metric, ocn_metric)


def spread_kernel(
    blocks, source_ref, returned_ref, select_ref, weight_ref, left_ref, right_ref, ends_ref, atm_hbm, ocn_hbm, out_ref,
    atm_ref, ocn_ref, row_ref, sems,
):
    copies = [
        pltpu.make_async_copy(atm_hbm, atm_ref, sems.at[0]),
        pltpu.make_async_copy(ocn_hbm, ocn_ref, sems.at[1]),
    ]
    for copy in copies:
        copy.start()
    tiles = weight_ref.shape[0]
    both = out_ref.shape[1]
    devs, per, _ = returned_ref.shape
    stack = returned_ref[...].reshape(devs * per, TILE)
    row_ref[...] = jnp.dot(select_ref[...], stack, preferred_element_type=F32)
    out_ref[...] = jnp.zeros_like(out_ref)

    def one_tile(tile, carry):
        block = lax.rem(source_ref[tile], blocks)
        back = lax.dot_general(
            row_ref[pl.ds(pl.multiple_of(both * tile, both), both)].astype(BF16),
            weight_ref[tile],
            (((1,), (1,)), ((), ())),
            preferred_element_type=F32,
        )
        out_ref[block] += back
        return carry

    lax.fori_loop(0, tiles, one_tile, 0, unroll=True)
    for copy in copies:
        copy.wait()
    levels, atm_rows, _ = atm_ref.shape
    fields, ocn_levels, columns = ocn_ref.shape
    first = levels * fields
    for halo, end, row, col in ((left_ref, 0, 0, 0), (right_ref, 1, atm_rows - fields, columns - TILE)):
        atm = step_size * jnp.dot(halo[:first], ends_ref[end, 0], preferred_element_type=F32)
        ocn = step_size * jnp.dot(halo[first:], ends_ref[end, 1], preferred_element_type=F32)
        for level in range(levels):
            atm_ref[level, row : row + fields, :] += atm[level * fields : (level + 1) * fields]
        for field in range(fields):
            ocn_ref[field, :, col : col + TILE] += ocn[field * ocn_levels : (field + 1) * ocn_levels]


def spreading(returned, tile_source, tile_weights, select, left, right, ends, atm_base, ocn_base, blocks, fields):
    tiles = tile_weights.shape[0]
    return pl.pallas_call(
        functools.partial(spread_kernel, blocks),
        out_shape=(
            jax.ShapeDtypeStruct((blocks, 2 * fields, TILE), F32),
            pltpu.VMEM(atm_base.shape, F32),
            pltpu.VMEM(ocn_base.shape, F32),
        ),
        in_specs=[in_smem()] + [in_vmem()] * 6 + [in_hbm()] * 2,
        out_specs=(in_vmem(),) * 3,
        scratch_shapes=[pltpu.VMEM((tiles * 2 * fields, TILE), F32), pltpu.SemaphoreType.DMA((2,))],
        compiler_params=limit(8),
        name="spreading",
    )(tile_source, returned, select, tile_weights, left, right, ends, outside(atm_base), outside(ocn_base))


def update_kernel(
    chunks, atm_ref, ocn_ref, own_ref, other_ref, atm_w, ocn_w, atm_out, ocn_out, atm_new, ocn_new, sems
):
    levels, atm_rows, _ = atm_ref.shape
    fields, ocn_levels, columns = ocn_ref.shape
    per = atm_rows // 8 // chunks
    wide = columns // chunks

    def out_of(chunk):
        rows = pl.ds(pl.multiple_of(chunk * 8 * per, 8), 8 * per)
        cols = pl.ds(pl.multiple_of(chunk * wide, TILE), wide)
        return [
            pltpu.make_async_copy(atm_new.at[:, rows, :], atm_out.at[:, rows, :], sems.at[chunk, 0]),
            pltpu.make_async_copy(ocn_new.at[:, :, cols], ocn_out.at[:, :, cols], sems.at[chunk, 1]),
        ]

    def one_chunk(chunk, carry):
        for inner in range(per):
            pair = chunk * per + inner
            flux = [flux_gain * (own_ref[2 * pair + half] + other_ref[2 * pair + half]) for half in range(2)]
            gain = jnp.concatenate([flux[0][:fields], flux[1][:fields]], axis=0)
            rows = pl.ds(pl.multiple_of(8 * pair, 8), 8)
            for level in range(levels):
                atm_new[level, rows, :] = atm_ref[level, rows, :] + atm_w[level] * gain
            for half in range(2):
                cols = pl.ds(pl.multiple_of((2 * pair + half) * TILE, TILE), TILE)
                for field in range(fields):
                    ocn_new[field, :, cols] = (
                        ocn_ref[field, :, cols] + ocn_w[...] * flux[half][fields + field : fields + field + 1]
                    )
        for copy in out_of(chunk):
            copy.start()
        return carry

    lax.fori_loop(0, chunks, one_chunk, 0)
    for chunk in range(chunks):
        for copy in out_of(chunk):
            copy.wait()


def update(atm_base, ocn_base, own, other, atm_wide, ocn_wide):
    chunks = 8
    return pl.pallas_call(
        functools.partial(update_kernel, chunks),
        out_shape=(
            jax.ShapeDtypeStruct(atm_base.shape, F32),
            jax.ShapeDtypeStruct(ocn_base.shape, F32),
        ),
        in_specs=[in_vmem()] * 6,
        out_specs=(in_hbm(),) * 2,
        scratch_shapes=[
            pltpu.VMEM(atm_base.shape, F32),
            pltpu.VMEM(ocn_base.shape, F32),
            pltpu.SemaphoreType.DMA((chunks, 2)),
        ],
        compiler_params=limit(12),
        name="update",
    )(held(atm_base), held(ocn_base), own, other, atm_wide, ocn_wide)


def neighbours(head, tail, axis):
    count = lax.axis_size(axis)
    if count % 2:
        onward = [(i, (i + 1) % count) for i in range(count)]
        return lax.ppermute(tail, axis, onward), lax.ppermute(head, axis, [(j, i) for i, j in onward])
    odd = lax.rem(lax.axis_index(axis), 2) == 1
    inner = [(i, i ^ 1) for i in range(count)]
    outer = [(i, (i - 1 if i % 2 == 0 else i + 1) % count) for i in range(count)]
    over_inner = lax.ppermute(jnp.where(odd, head, tail), axis, inner)
    over_outer = lax.ppermute(jnp.where(odd, tail, head), axis, outer)
    return jnp.where(odd, over_inner, over_outer), jnp.where(odd, over_outer, over_inner)


def routes(tile_source, tile_target, owner_map, blocks, fields, dev_count):
    tiles = tile_source.shape[0]
    xblocks = owner_map.shape[0]
    per = fields * CAP
    matched = tile_target[:, None] == jnp.arange(xblocks, dtype=jnp.int32)[None, :]
    placed_at = jnp.sum(jnp.where(matched, owner_map[None, :], 0), axis=1)
    owner = placed_at // XB_DEV
    side = (tile_source >= blocks).astype(jnp.int32)
    segment = side * XB_DEV + placed_at % XB_DEV
    index = jnp.arange(tiles, dtype=jnp.int32)
    before = (index[None, :] < index[:, None]) & (owner[None, :] == owner[:, None])
    rank = jnp.sum(before.astype(jnp.int32), axis=1)
    slots = jnp.arange(dev_count * 8, dtype=jnp.int32)
    at_slot = (slots[:, None] // 8 == owner[None, :]) & (slots[:, None] % CAP == rank[None, :])
    label = jnp.sum(jnp.where(at_slot, segment[None, :] + 1, 0), axis=1) - 1
    labels = jnp.broadcast_to(label.astype(F32)[:, None], (dev_count * 8, TILE)).reshape(dev_count, 8, TILE)
    field = jnp.arange(fields, dtype=jnp.int32)
    goes = jnp.where(
        side[:, None, None] == jnp.arange(2, dtype=jnp.int32)[None, :, None],
        (owner * per + rank)[:, None, None] + field[None, None, :] * CAP,
        -1,
    ).reshape(tiles * 2 * fields)
    rows = jnp.arange(dev_count * per, dtype=jnp.int32)
    to_slots = (rows[:, None] == goes[None, :]).astype(BF16)
    to_tiles = (goes[:, None] == rows[None, :]).astype(BF16)
    return labels, to_slots, to_tiles


def shards(
    atm_state,
    ocn_state,
    atm_weights,
    ocn_weights,
    atm_metric,
    ocn_metric,
    atm_links,
    ocn_links,
    tile_weights,
    tile_source,
    tile_target,
    owner_map,
):
    comp_count = lax.axis_size("comp")
    dev_count = comp_count * lax.axis_size("lev")
    fields, _, columns = atm_state.shape
    blocks = columns // TILE
    swap = [(0, 1), (1, 0)]

    atm_rows = to_rows(atm_state)
    part, head, tail, atm_wide, ocn_wide = surface(atm_rows, ocn_state, atm_weights, ocn_weights)
    part_other = lax.ppermute(part, "lev", swap)
    labels, to_slots, to_tiles = routes(tile_source, tile_target, owner_map, blocks, fields, dev_count)
    outgoing = contributions(part, part_other, tile_source, tile_weights, to_slots, labels)
    start = (lax.axis_index("comp") * columns).astype(jnp.int32).reshape(1)
    outgoing, start = lax.optimization_barrier((outgoing, start))
    arrived = lax.all_to_all(outgoing, BOTH, split_axis=0, concat_axis=0, tiled=True)
    atm_base, ocn_base, ends = diffusion(
        start, columns * comp_count, atm_rows, ocn_state, atm_links, ocn_links, atm_metric, ocn_metric
    )
    arrived, atm_base, ocn_base, ends = lax.optimization_barrier((arrived, atm_base, ocn_base, ends))
    xgrid, answer = fluxes(arrived, fields)
    answer, head, tail = lax.optimization_barrier((answer, head, tail))
    returned = lax.all_to_all(answer, BOTH, split_axis=0, concat_axis=0, tiled=True)
    left, right = neighbours(head, tail, "comp")
    returned, left, right = lax.optimization_barrier((returned, left, right))
    spread, atm_base, ocn_base = spreading(
        returned, tile_source, tile_weights, to_tiles, left, right, ends, atm_base, ocn_base, blocks, fields
    )
    spread_other = lax.ppermute(spread, "lev", swap)
    atm_new, ocn_new = update(atm_base, ocn_base, spread, spread_other, atm_wide, ocn_wide)
    return (from_rows(atm_new, fields), ocn_new, xgrid)


def solution(mesh):
    placed = (
        P(None, "lev", ("grp", "comp")),
        P(None, "lev", ("grp", "comp")),
        P("lev"),
        P("lev"),
        P(None, "comp"),
        P(None, "comp"),
        P(None, "comp"),
        P(None, "comp"),
        P(("comp", "lev"), None, None),
        P(("comp", "lev")),
        P(("comp", "lev")),
        P(),
    )
    return jax.shard_map(
        shards,
        mesh=mesh,
        in_specs=placed,
        out_specs=(
            P(None, "lev", ("grp", "comp")),
            P(None, "lev", ("grp", "comp")),
            P(("grp", "comp", "lev"), None, None),
        ),
        check_vma=False,
    )
```

time: 208 us -> 50.8 us (0.24)
  local copies, waits for them, and re-layouts: 84 us -> 0.33 us
  matrix products: 41.5 us -> 0 us
  other arithmetic: 37.7 us -> 1.01 us
  Pallas kernels: 0 us -> 24.2 us
  between operations: 14.5 us -> 0.89 us
  waiting for transfers between devices: 0.03 us -> 8.17 us
  starting transfers between devices: 24 us -> 15.9 us
  blocking collectives: 4.73 us -> 0 us
    dot_general x13 -> x0, matrix products: 28.6 us -> none  [the longest x1 15 us: diffuse(): jnp.einsum('flbw,bcw->flbc', windows, operator, precision=lax.Precision.H...]
    pallas_call x0 -> x6, Pallas kernels: none -> 24.2 us  [the longest x1 11.2 us: diffusion(): pl.pallas_call(functools.partial(diffuse_kernel, all_cols), out_shape=(pl...]
    slice x7 -> x0, local copies, waits for them, and re-layouts: 21.8 us -> none  [the longest x1 11.6 us: block_windows(): extended[:, :, 2 * HALO:2 * HALO + columns]]
    unnamed x63 -> x16, local copies, waits for them, and re-layouts: 21.5 us -> 0.04 us
    reshape x8 -> x0, local copies, waits for them, and re-layouts: 20.7 us -> none  [the longest x1 5.48 us: block_windows(): left = extended[:, :, :columns].reshape(fields, levels, blocks, tile_size)]
    unnamed x1 -> x0, matrix products: 12.9 us -> none
    add x4 -> x3, other arithmetic: 9.95 us -> 0.09 us  [the longest x1 0.07 us: routes(): (owner * per + rank)[:, None, None] + field[None, None, :] * CAP]
    unnamed x1 -> x0, other arithmetic: 8.74 us -> none
  transfers between devices with their start and end apart: 6 -> 6, of which waited for: 0 -> 3; matrix products, arithmetic and copies ran while one was open for 69% -> 2% of each run, Pallas kernels for 0% -> 22%
where the time goes in v1:
time: 50.8 us; the launch traced here: 50.5 us
  Pallas kernels  24.2 us (48%)
  starting transfers between devices  15.9 us (31%)
  waiting for transfers between devices  8.17 us (16%)
  other arithmetic  1.01 us (2%)
  between operations  0.89 us (2%)
    pallas_call x1, Pallas kernels, diffusion(): pl.pallas_call(functools.partial(diffuse_kernel, all_cols), out_shape=(pl...  11.2 us
    all_to_all x1, starting transfers between devices, shards(): lax.all_to_all(outgoing, BOTH, split_axis=0, concat_axis=0, tiled=True)  7.14 us
    all_to_all x1, waiting for transfers between devices, shards(): lax.all_to_all(answer, BOTH, split_axis=0, concat_axis=0, tiled=True)  6.07 us
    ppermute x1, starting transfers between devices, neighbours(): over_outer = lax.ppermute(jnp.where(odd, tail, head), axis, outer)  4.69 us
    pallas_call x1, Pallas kernels, spreading(): pl.pallas_call(functools.partial(spread_kernel, blocks), out_shape=(jax.S...  4.44 us
    all_to_all x1, starting transfers between devices, shards(): lax.all_to_all(answer, BOTH, split_axis=0, concat_axis=0, tiled=True)  3.51 us
    pallas_call x1, Pallas kernels, surface(): pl.pallas_call(functools.partial(surface_kernel, chunks), out_shape=(jax....  2.91 us
    pallas_call x1, Pallas kernels, update(): pl.pallas_call(functools.partial(update_kernel, chunks), out_shape=(jax.S...  2.5 us
  transfers between devices with their start and end apart: 6, of which 3 were waited for; matrix products, arithmetic and copies ran while one was open for 2% of the time, Pallas kernels for 22%

profile of v1, /device:TPU:0, one launch (start us, length us, event | category | flops | bytes accessed | tf_op | source)
XLA Modules:
  0.0 50.5 jit_solution(4843728691886410358)
XLA Ops:
  0.6 0.0 copy-start.5
  0.6 0.0 copy-start.6
  0.7 0.0 copy-start.7
  0.7 0.0 copy-start
  0.7 2.9 %surface.1 = (f32[32,8,128]{2,1,0:T(8,128)S(1)}, bf16[304,128]{1,0:T(8,128)(2,1)S(1)}, bf16[304,128]{1,0:T(8,128)(2,1)S(1)}, f32[36,8,128]{2,1,0:T(8,128)S(1)}, f32[40,128]{1,0:T(8,128)S(1)}) custom-call(f32[36,128,128]{2,1,0:T(8,128)} %bitcast.15, f32[4,40,4096]{2,1,0:T(8,128)} %ocn_hbm.3, f32[36]{0:T(128)} %atm_w.1, f32[40]{0:T(128)} %ocn_w.1), custom_call_target="tpu_custom_call" | custom-call | tf_op jit(solution)/shard_map/surface/pallas_call | solution.py:119
  3.6 0.0 copy-start.1
  3.6 0.0 copy-start.2
  3.6 0.0 copy-start.3
  3.6 0.0 copy-start.4
  3.6 0.5 %collective-permute-start = (f32[32,8,128]{2,1,0:T(8,128)S(1)}, f32[32,8,128]{2,1,0:T(8,128)S(1)}, u32[]{:S(2)}, u32[]{:S(2)}) collective-permute-start(f32[32,8,128]{2,1,0:T(8,128)S(1)} %get-tuple-element.30.own_ref), channel_id=1, source_target_pairs={{0,1},{1,0},{2,3},{3,2},{4,5},{5,4},{6,7},{7,6},{8,9},{9,8},{10,11... | collective-permute-start | bytes 393224 | tf_op jit(solution)/shard_map/ppermute | solution.py:596
  4.2 0.0 copy-done.5
  4.2 0.0 copy-done.6
  4.2 0.0 copy-done.7
  4.2 0.2 select_reduce_fusion
  4.4 0.2 convert_reduce_fusion
  4.6 0.1 select_reduce_fusion.1
  4.7 0.1 convert_element_type.26
  4.8 0.1 iota_compare_fusion.4
  4.9 0.1 broadcast_add_fusion
  4.9 0.1 broadcast_select_fusion.4
  5.1 0.1 select_n.91
  5.2 0.1 fusion.select_ref
  5.3 0.0 collective-permute-done.other_ref
  5.3 0.1 broadcast_in_dim.75.label_ref
  5.4 0.0 copy-done
  5.4 2.0 %contributions.1 = bf16[16,24,128]{2,1,0:T(8,128)(2,1)} custom-call(s32[64]{0:T(128)S(1)} %copy-done.5, f32[32,8,128]{2,1,0:T(8,128)S(1)} %get-tuple-element.30.own_ref, f32[32,8,128]{2,1,0:T(8,128)S(1)} %collective-permute-done.other_ref, bf16[64,128,128]{2,1,0:T(8,128)(2,1)S(1)} %copy-done, bf16[256,512]{1,0:T(8,128)(2,1)S(1)} %fusion.select_ref, ...), custom_call_target="tpu_custom_call" | custom-call | tf_op jit(solution)/shard_map/contributions/pallas_call | solution.py:166
  7.4 7.1 %all-to-all-start = ((bf16[16,24,128]{2,1,0:T(8,128)(2,1)}), bf16[16,24,128]{2,1,0:T(8,128)(2,1)S(1)}, u32[]{:S(2)}, u32[]{:S(2)}) async-start(bf16[16,24,128]{2,1,0:T(8,128)(2,1)} %contributions.1), calls=%async_computation | async-start | bytes 196608 | tf_op jit(solution)/shard_map/all_to_all | solution.py:601
  14.6 0.0 copy-done.1
  14.6 0.0 copy-done.2
  14.6 0.0 copy-done.3
  14.6 0.0 copy-done.4
  14.6 11.2 %diffusion.1 = (f32[36,128,128]{2,1,0:T(8,128)}, f32[4,40,4096]{2,1,0:T(8,128)}, bf16[2,2,128,128]{3,2,1,0:T(8,128)(2,1)S(1)}) custom-call(s32[1]{0:T(128)} %bitcast.4.start_ref, f32[36,128,128]{2,1,0:T(8,128)} %bitcast.16, f32[4,40,4096]{2,1,0:T(8,128)} %ocn_hbm.3, s32[4,4096]{1,0:T(4,128)S(1)} %copy-done.3, s32[6,4096]{1,0:T(8,128)S(1)} %copy-done.1, ...), custom_call_target="tpu_custom_call" | custom-call | tf_op jit(solution)/shard_map/diffusion/pallas_call | solution.py:387
  25.9 0.0 all-to-all-done.arrived_ref
  25.9 1.0 %fluxes.1 = (bf16[16,8,128]{2,1,0:T(8,128)(2,1)}, bf16[16,16,128]{2,1,0:T(8,128)(2,1)}) custom-call(bf16[16,24,128]{2,1,0:T(8,128)(2,1)S(1)} %all-to-all-done.arrived_ref), custom_call_target="tpu_custom_call" | custom-call | tf_op jit(solution)/shard_map/fluxes/pallas_call | solution.py:221
  26.9 4.7 %collective-permute-start.2 = (bf16[304,128]{1,0:T(8,128)(2,1)S(1)}, bf16[304,128]{1,0:T(8,128)(2,1)S(1)}, u32[]{:S(2)}, u32[]{:S(2)}) collective-permute-start(bf16[304,128]{1,0:T(8,128)(2,1)S(1)} %get-tuple-element.59), channel_id=1, source_target_pairs={{0,14},{2,4},{4,2},{6,8},{8,6},{10,12},{12,10},{14,0},{1,15},{3,5}... | collective-permute-start | bytes 233480 | tf_op jit(solution)/shard_map/ppermute | solution.py:542
  31.6 0.0 collective-permute-start.1
  31.6 0.1 fusion.1.select_ref
  31.8 3.5 %all-to-all-start.1 = ((bf16[16,16,128]{2,1,0:T(8,128)(2,1)}), bf16[16,16,128]{2,1,0:T(8,128)(2,1)S(1)}, u32[]{:S(2)}, u32[]{:S(2)}) async-start(bf16[16,16,128]{2,1,0:T(8,128)(2,1)} %get-tuple-element.40), calls=%async_computation.1 | async-start | bytes 131072 | tf_op jit(solution)/shard_map/all_to_all | solution.py:608
  35.3 0.0 collective-permute-done.2
  35.3 0.8 %collective-permute-done.1 = bf16[304,128]{1,0:T(8,128)(2,1)S(1)} collective-permute-done((bf16[304,128]{1,0:T(8,128)(2,1)S(1)}, bf16[304,128]{1,0:T(8,128)(2,1)S(1)}, u32[]{:S(2)}, u32[]{:S(2)}) %collective-permute-start.1) | collective-permute-done | bytes 77856 | tf_op jit(solution)/shard_map/ppermute | solution.py:541
  36.1 6.1 %all-to-all-done.1.returned_ref = bf16[16,16,128]{2,1,0:T(8,128)(2,1)S(1)} async-done(((bf16[16,16,128]{2,1,0:T(8,128)(2,1)}), bf16[16,16,128]{2,1,0:T(8,128)(2,1)S(1)}, u32[]{:S(2)}, u32[]{:S(2)}) %all-to-all-start.1) | async-done | bytes 65568 | tf_op jit(solution)/shard_map/all_to_all | solution.py:608
  42.1 4.4 %spreading.1 = (f32[32,8,128]{2,1,0:T(8,128)S(1)}, f32[36,128,128]{2,1,0:T(8,128)S(1)}, f32[4,40,4096]{2,1,0:T(8,128)S(1)}) custom-call(s32[64]{0:T(128)S(1)} %copy-done.5, bf16[16,16,128]{2,1,0:T(8,128)(2,1)S(1)} %all-to-all-done.1.returned_ref, bf16[512,256]{1,0:T(8,128)(2,1)S(1)} %fusion.1.select_ref, bf16[64,128,128]{2,1,0:T(8,128)(2,1)S(1)} %copy-done, ...), custom_call_target="tpu_custom_call" | custom-call | tf_op jit(solution)/shard_map/spreading/pallas_call | solution.py:458
  46.6 0.1 collective-permute-start.3
  46.7 1.3 %collective-permute-done.3.other_ref = f32[32,8,128]{2,1,0:T(8,128)S(1)} collective-permute-done((f32[32,8,128]{2,1,0:T(8,128)S(1)}, f32[32,8,128]{2,1,0:T(8,128)S(1)}, u32[]{:S(2)}, u32[]{:S(2)}) %collective-permute-start.3) | collective-permute-done | bytes 131104 | tf_op jit(solution)/shard_map/ppermute | solution.py:614
  48.0 2.5 %update.1 = (f32[36,128,128]{2,1,0:T(8,128)}, f32[4,40,4096]{2,1,0:T(8,128)}) custom-call(f32[36,128,128]{2,1,0:T(8,128)S(1)} %get-tuple-element.49.atm_ref, f32[4,40,4096]{2,1,0:T(8,128)S(1)} %get-tuple-element.50.ocn_ref, f32[32,8,128]{2,1,0:T(8,128)S(1)} %get-tuple-element.51.own_ref, f32[32,8,128]{2,1,0:T(8,128)S(1)} %collective-permute-done.3.other_ref, ...), custom_call_target="tpu_custom_call" | custom-call | tf_op jit(solution)/shard_map/update/pallas_call | solution.py:515
  (8 shorter events, 0.1 us)
Async XLA Ops:
  0.6 3.5 %copy-start.5 = (s32[64]{0:T(128)S(1)}, s32[64]{0:T(128)}, u32[]{:S(2)}) copy-start(s32[64]{0:T(128)} %source_ref.3) | copy-start | bytes 772
  0.6 3.5 %copy-start.6 = (s32[256]{0:T(256)S(1)}, s32[256]{0:T(256)}, u32[]{:S(2)}) copy-start(s32[256]{0:T(256)} %param.23) | copy-start | bytes 3076
  0.7 3.5 %copy-start.7 = (s32[64]{0:T(128)S(1)}, s32[64]{0:T(128)}, u32[]{:S(2)}) copy-start(s32[64]{0:T(128)} %param.22) | copy-start | bytes 772
  0.7 4.7 %copy-start = (bf16[64,128,128]{2,1,0:T(8,128)(2,1)S(1)}, bf16[64,128,128]{2,1,0:T(8,128)(2,1)}, u32[]{:S(2)}) copy-start(bf16[64,128,128]{2,1,0:T(8,128)(2,1)} %weight_ref.3) | copy-start | bytes 6291460
  3.6 11.0 %copy-start.1 = (s32[6,4096]{1,0:T(8,128)S(1)}, s32[6,4096]{1,0:T(8,128)}, u32[]{:S(2)}) copy-start(s32[6,4096]{1,0:T(8,128)} %ocn_links.1) | copy-start | bytes 294916
  3.6 11.0 %copy-start.2 = (f32[6,4096]{1,0:T(8,128)S(1)}, f32[6,4096]{1,0:T(8,128)}, u32[]{:S(2)}) copy-start(f32[6,4096]{1,0:T(8,128)} %ocn_metric.1) | copy-start | bytes 294916
  3.6 11.0 %copy-start.3 = (s32[4,4096]{1,0:T(4,128)S(1)}, s32[4,4096]{1,0:T(4,128)}, u32[]{:S(2)}) copy-start(s32[4,4096]{1,0:T(4,128)} %atm_links.1) | copy-start | bytes 196612
  3.6 11.0 %copy-start.4 = (f32[4,4096]{1,0:T(4,128)S(1)}, f32[4,4096]{1,0:T(4,128)}, u32[]{:S(2)}) copy-start(f32[4,4096]{1,0:T(4,128)} %atm_metric.1) | copy-start | bytes 196612
  3.6 1.6 %collective-permute-start = (f32[32,8,128]{2,1,0:T(8,128)S(1)}, f32[32,8,128]{2,1,0:T(8,128)S(1)}, u32[]{:S(2)}, u32[]{:S(2)}) collective-permute-start(f32[32,8,128]{2,1,0:T(8,128)S(1)} %get-tuple-element.30.own_ref), channel_id=1, source_target_pairs={{0,1},{1,0},{2,3},{3,2},{4,5},{5,4},{6,7},{7,6},{8,9},{9,8},{10,11... | collective-permute-start | bytes 393224 | tf_op jit(solution)/shard_map/ppermute | solution.py:596
  7.4 18.4 %all-to-all-start = ((bf16[16,24,128]{2,1,0:T(8,128)(2,1)}), bf16[16,24,128]{2,1,0:T(8,128)(2,1)S(1)}, u32[]{:S(2)}, u32[]{:S(2)}) async-start(bf16[16,24,128]{2,1,0:T(8,128)(2,1)} %contributions.1), calls=%async_computation | async-start | bytes 196608 | tf_op jit(solution)/shard_map/all_to_all | solution.py:601
  26.9 8.4 %collective-permute-start.2 = (bf16[304,128]{1,0:T(8,128)(2,1)S(1)}, bf16[304,128]{1,0:T(8,128)(2,1)S(1)}, u32[]{:S(2)}, u32[]{:S(2)}) collective-permute-start(bf16[304,128]{1,0:T(8,128)(2,1)S(1)} %get-tuple-element.59), channel_id=1, source_target_pairs={{0,14},{2,4},{4,2},{6,8},{8,6},{10,12},{12,10},{14,0},{1,15},{3,5}... | collective-permute-start | bytes 233480 | tf_op jit(solution)/shard_map/ppermute | solution.py:542
  31.6 4.4 %collective-permute-start.1 = (bf16[304,128]{1,0:T(8,128)(2,1)S(1)}, bf16[304,128]{1,0:T(8,128)(2,1)S(1)}, u32[]{:S(2)}, u32[]{:S(2)}) collective-permute-start(bf16[304,128]{1,0:T(8,128)(2,1)S(1)} %get-tuple-element.60), channel_id=1, source_target_pairs={{0,2},{2,0},{4,6},{6,4},{8,10},{10,8},{12,14},{14,12},{1,3},{3,1},... | collective-permute-start | bytes 233480 | tf_op jit(solution)/shard_map/ppermute | solution.py:541
  31.8 10.4 %all-to-all-start.1 = ((bf16[16,16,128]{2,1,0:T(8,128)(2,1)}), bf16[16,16,128]{2,1,0:T(8,128)(2,1)S(1)}, u32[]{:S(2)}, u32[]{:S(2)}) async-start(bf16[16,16,128]{2,1,0:T(8,128)(2,1)} %get-tuple-element.40), calls=%async_computation.1 | async-start | bytes 131072 | tf_op jit(solution)/shard_map/all_to_all | solution.py:608
  46.6 1.4 %collective-permute-start.3 = (f32[32,8,128]{2,1,0:T(8,128)S(1)}, f32[32,8,128]{2,1,0:T(8,128)S(1)}, u32[]{:S(2)}, u32[]{:S(2)}) collective-permute-start(f32[32,8,128]{2,1,0:T(8,128)S(1)} %get-tuple-element.51.own_ref), channel_id=1, source_target_pairs={{0,1},{1,0},{2,3},{3,2},{4,5},{5,4},{6,7},{7,6},{8,9},{9,8},{10,11... | collective-permute-start | bytes 393224 | tf_op jit(solution)/shard_map/ppermute | solution.py:614

commit v2 on v1

v2 whole, which is shorter than its diff:
```python
import functools

import jax
import jax.numpy as jnp
from jax import lax
from jax.experimental import pallas as pl
from jax.experimental.pallas import tpu as pltpu
from jax.sharding import PartitionSpec as P

HALO = 128
CAP = 4
XB_DEV = 16
TILE = 128
step_size = 1.0
flux_gain = 10.0
BF16 = jnp.bfloat16
F32 = jnp.float32
BOTH = ("comp", "lev")


def in_vmem():
    return pl.BlockSpec(memory_space=pltpu.VMEM)


def in_smem():
    return pl.BlockSpec(memory_space=pltpu.SMEM)


def in_hbm():
    return pl.BlockSpec(memory_space=pl.ANY)


def held(array):
    return pltpu.with_memory_space_constraint(array, pltpu.VMEM)


def outside(array):
    return pltpu.with_memory_space_constraint(array, pltpu.HBM)


def limit(mib):
    return pltpu.CompilerParams(vmem_limit_bytes=mib * 1024 * 1024)


def to_rows(state):
    fields, levels, columns = state.shape
    blocks = columns // TILE
    split = state.transpose(1, 0, 2).reshape(levels, fields, blocks, TILE)
    return split.transpose(0, 2, 1, 3).reshape(levels, blocks * fields, TILE)


def from_rows(rows, fields):
    levels, count, _ = rows.shape
    blocks = count // fields
    split = rows.reshape(levels, blocks, fields, TILE).transpose(0, 2, 1, 3)
    return split.reshape(levels, fields, blocks * TILE).transpose(1, 0, 2)


def upper_half(fields):
    return lax.broadcasted_iota(jnp.int32, (8, TILE), 0) < fields


def turned(rows):
    return pltpu.roll(rows, 4, 0)


def halves(atm_ref, row, top):
    rows = [[], []]
    for level in range(0, atm_ref.shape[0], 2):
        low, high = atm_ref[level, pl.ds(row, 8), :], atm_ref[level + 1, pl.ds(row, 8), :]
        rows[0].append(jnp.where(top, low, turned(high)))
        rows[1].append(jnp.where(top, turned(low), high))
    return [jnp.concatenate(part, axis=0) for part in rows]


def over_lanes(values_ref, out_ref):
    for level in range(out_ref.shape[0]):
        out_ref[level : level + 1] = jnp.full((1, TILE), values_ref[level], F32)


def surface_kernel(
    chunks, paired, atm_hbm, ocn_hbm, atm_w, ocn_w, part_ref, inner_ref, outer_ref, atm_wide_hbm,
    ocn_wide_hbm, atm_ref, ocn_ref, ends_ref, atm_wide, ocn_wide, atm_s, ocn_s, sems, few_sems, wide_sems,
):
    levels, atm_rows, _ = atm_ref.shape
    fields, ocn_levels, columns = ocn_ref.shape
    deep = atm_rows // chunks
    wide = columns // chunks
    top = upper_half(fields)
    copies = []
    for chunk in range(chunks):
        rows = pl.ds(chunk * deep, deep)
        cols = pl.ds(chunk * wide, wide)
        for which, (src, dst) in enumerate(
            ((atm_hbm.at[:, rows, :], atm_ref.at[:, rows, :]), (ocn_hbm.at[:, :, cols], ocn_ref.at[:, :, cols]))
        ):
            copy = pltpu.make_async_copy(src, dst, sems.at[chunk, which])
            copy.start()
            copies.append(copy)
    few = [
        pltpu.make_async_copy(atm_w, atm_s, few_sems.at[0]),
        pltpu.make_async_copy(ocn_w, ocn_s, few_sems.at[1]),
    ]
    for copy in few:
        copy.start()
    for copy in few:
        copy.wait()
    over_lanes(atm_s, atm_wide)
    over_lanes(ocn_s, ocn_wide)
    wides = [
        pltpu.make_async_copy(atm_wide, atm_wide_hbm, wide_sems.at[0]),
        pltpu.make_async_copy(ocn_wide, ocn_wide_hbm, wide_sems.at[1]),
    ]
    for copy in wides:
        copy.start()
    for chunk in range(chunks):
        copies[2 * chunk].wait()
        copies[2 * chunk + 1].wait()

        def one_pair(pair, carry):
            rows = pl.ds(pl.multiple_of(pair * 8, 8), 8)
            atm = atm_ref[0, rows, :] * atm_wide[:1]
            for level in range(1, levels):
                atm = atm + atm_ref[level, rows, :] * atm_wide[level : level + 1]
            for half in range(2):
                block = 2 * pair + half
                cols = pl.ds(pl.multiple_of(block * TILE, TILE), TILE)
                ocn = [
                    jnp.sum(ocn_ref[field, :, cols] * ocn_wide[...], axis=0, keepdims=True) for field in range(fields)
                ]
                part_ref[block] = jnp.concatenate([atm[half * fields : (half + 1) * fields]] + ocn, axis=0)
            return carry

        lax.fori_loop(chunk * (deep // 8), (chunk + 1) * (deep // 8), one_pair, 0)
    ends_ref[0] = jnp.concatenate(
        [halves(atm_ref, 0, top)[0]] + [ocn_ref[field, :, :HALO] for field in range(fields)], axis=0
    ).astype(BF16)
    ends_ref[1] = jnp.concatenate(
        [halves(atm_ref, atm_rows - 8, top)[1]] + [ocn_ref[field, :, columns - HALO :] for field in range(fields)], axis=0
    ).astype(BF16)
    first_block = lax.rem(lax.axis_index("comp"), 2) if paired else 0
    inner_ref[...] = ends_ref[1 - first_block]
    outer_ref[...] = ends_ref[first_block]
    for copy in wides:
        copy.wait()


def surface(atm_rows, ocn_state, atm_weights, ocn_weights, paired):
    levels, count, _ = atm_rows.shape
    fields, ocn_levels, columns = ocn_state.shape
    rows = fields * (levels + ocn_levels)
    chunks = 4
    return pl.pallas_call(
        functools.partial(surface_kernel, chunks, paired),
        out_shape=(
            jax.ShapeDtypeStruct((columns // TILE, 2 * fields, TILE), F32),
            jax.ShapeDtypeStruct((rows, HALO), BF16),
            jax.ShapeDtypeStruct((rows, HALO), BF16),
            pltpu.HBM((levels, TILE), F32),
            pltpu.HBM((ocn_levels, TILE), F32),
        ),
        in_specs=[in_hbm()] * 4,
        out_specs=(in_vmem(),) * 3 + (in_hbm(),) * 2,
        scratch_shapes=[
            pltpu.VMEM(atm_rows.shape, F32),
            pltpu.VMEM(ocn_state.shape, F32),
            pltpu.VMEM((2, rows, HALO), BF16),
            pltpu.VMEM((levels, TILE), F32),
            pltpu.VMEM((ocn_levels, TILE), F32),
            pltpu.SMEM((levels,), F32),
            pltpu.SMEM((ocn_levels,), F32),
            pltpu.SemaphoreType.DMA((chunks, 2)),
            pltpu.SemaphoreType.DMA((2,)),
            pltpu.SemaphoreType.DMA((2,)),
        ],
        compiler_params=limit(12),
        name="surface",
    )(outside(atm_rows), outside(ocn_state), outside(atm_weights), outside(ocn_weights))


def contrib_kernel(
    blocks, source_ref, own_ref, other_ref, weight_ref, select_ref, label_ref, out_ref, surf_ref, row_ref
):
    surf_ref[...] = (own_ref[...] + other_ref[...]).astype(BF16).astype(F32)
    tiles = weight_ref.shape[0]
    both = own_ref.shape[1]
    devs, depth, _ = out_ref.shape

    for tile in range(tiles):
        block = lax.rem(source_ref[tile], blocks)
        row_ref[both * tile : both * (tile + 1)] = jnp.dot(
            surf_ref[block].astype(BF16), weight_ref[tile], preferred_element_type=F32
        )
    placed = jnp.dot(select_ref[...], row_ref[...].astype(BF16), preferred_element_type=F32)
    placed = placed.reshape(devs, depth - 8, TILE)
    out_ref[...] = jnp.concatenate([placed, label_ref[...]], axis=1).astype(BF16)


def contributions(own, other, tile_source, tile_weights, select, labels):
    blocks, both, _ = own.shape
    tiles = tile_weights.shape[0]
    devs = labels.shape[0]
    return pl.pallas_call(
        functools.partial(contrib_kernel, blocks),
        out_shape=jax.ShapeDtypeStruct((devs, CAP * both // 2 + 8, TILE), BF16),
        in_specs=[in_smem()] + [in_vmem()] * 5,
        out_specs=in_vmem(),
        scratch_shapes=[pltpu.VMEM(own.shape, F32), pltpu.VMEM((tiles * both, TILE), F32)],
        compiler_params=limit(8),
        name="contributions",
    )(tile_source, own, other, tile_weights, select, labels)


def bulk_fluxes(air, sea):
    shear_u = air[2] - sea[2]
    shear_v = air[3] - sea[3]
    wind_speed = jnp.sqrt(shear_u * shear_u + shear_v * shear_v + 1.0)
    stress_u = 0.8 * wind_speed * shear_u
    stress_v = 0.8 * wind_speed * shear_v
    sensible = 0.6 * wind_speed * (sea[0] - air[0])
    saturated = 0.6 * jnp.exp(0.3 * sea[0]) * (1.0 - 0.1 * jnp.tanh(sea[1]))
    latent = 0.5 * wind_speed * (saturated - air[1])
    return (
        [sensible, latent, -stress_u, -stress_v],
        [-(sensible + latent), latent, stress_u, stress_v],
    )


def flux_kernel(fields, arrived_ref, grid_ref, answer_ref):
    devs, depth, _ = arrived_ref.shape
    per = fields * CAP
    arrived = arrived_ref[...].astype(F32)
    values = arrived[:, :per].reshape(devs * per, TILE).astype(BF16)
    labels = jnp.concatenate([arrived[:, per:]] * (per // 8), axis=1)
    field = lax.broadcasted_iota(jnp.int32, labels.shape, 1) // CAP
    codes = (labels + (field * (2 * XB_DEV)).astype(F32)).reshape(devs * per, TILE)
    codes = jnp.where(labels.reshape(devs * per, TILE) < 0.0, -1.0, codes)
    lane = lax.broadcasted_iota(jnp.int32, (1, TILE), 1)
    side, rest = lane // (fields * XB_DEV), lane % (fields * XB_DEV)
    code_of = side * XB_DEV + rest % XB_DEV + rest // XB_DEV * (2 * XB_DEV)
    hot = jnp.where(codes == code_of.astype(F32), 1.0, 0.0).astype(BF16)
    sums = lax.dot_general(hot, values, (((0,), (0,)), ((), ())), preferred_element_type=F32)
    rows = [sums[XB_DEV * k : XB_DEV * (k + 1)] for k in range(2 * fields)]
    atm_flux, ocn_flux = bulk_fluxes(rows[:fields], rows[fields:])
    table = jnp.concatenate(atm_flux + ocn_flux, axis=0).astype(BF16)
    to = lax.broadcasted_iota(jnp.int32, (TILE, TILE), 0)
    at = lax.broadcasted_iota(jnp.int32, (TILE, TILE), 1)
    both = 2 * fields
    moves = jnp.where(at == to % both * XB_DEV + to // both, 1.0, 0.0).astype(BF16)
    moved = jnp.dot(moves, table, preferred_element_type=F32)
    grid_ref[...] = moved.reshape(XB_DEV, both, TILE).astype(BF16)
    answer = jnp.dot(hot, table, preferred_element_type=F32)
    answer_ref[...] = answer.reshape(devs, per, TILE).astype(BF16)


def fluxes(arrived, fields):
    devs, _, _ = arrived.shape
    return pl.pallas_call(
        functools.partial(flux_kernel, fields),
        out_shape=(
            jax.ShapeDtypeStruct((XB_DEV, 2 * fields, TILE), BF16),
            jax.ShapeDtypeStruct((devs, fields * CAP, TILE), BF16),
        ),
        in_specs=[in_vmem()],
        out_specs=(in_vmem(),) * 2,
        compiler_params=limit(8),
        name="fluxes",
    )(arrived)


def fill_operator(out, grid_ref, links, metric, cols, first_col, all_cols):
    edges = links.shape[0]
    lane = lax.broadcasted_iota(jnp.int32, (edges, TILE), 1)
    away = links[:, cols] - (first_col + lane)
    away = jnp.where(away > all_cols // 2, away - all_cols, away)
    away = jnp.where(away < -(all_cols // 2), away + all_cols, away)
    place = (away + lane).astype(F32)
    value = step_size * metric[:, cols]
    keep = 1.0 - jnp.sum(value, axis=0, keepdims=True)
    place = jnp.concatenate([place, jnp.full((8 - edges, TILE), -1.0e6, F32)], axis=0)
    value = jnp.concatenate([value, jnp.zeros((8 - edges, TILE), F32)], axis=0)
    edge = lax.broadcasted_iota(jnp.int32, (8, TILE), 0)
    whole = value
    for back in range(1, edges):
        same = (pltpu.roll(place, back, 0) == place) & (edge >= back)
        whole = whole + jnp.where(same, pltpu.roll(value, back, 0), 0.0)
    places = [jnp.broadcast_to(place[k : k + 1], (16, TILE)).astype(BF16) for k in range(edges)]
    sums = [jnp.broadcast_to(whole[k : k + 1], (16, TILE)).astype(BF16) for k in range(edges)]
    lanes = lax.broadcasted_iota(jnp.int32, (16, TILE), 1).astype(F32).astype(BF16)
    keep = jnp.broadcast_to(keep, (16, TILE)).astype(BF16)
    for group in range((TILE + 2 * HALO) // 16):
        here = grid_ref[16 * group : 16 * (group + 1)]
        found = jnp.zeros((16, TILE), BF16)
        if HALO <= 16 * group < HALO + TILE:
            found = jnp.where(lanes == here, keep, found)
        for k in range(edges):
            found = jnp.where(places[k] == here, sums[k], found)
        out[16 * group : 16 * (group + 1)] = found


def place_grid(grid_ref):
    grid_ref[...] = (lax.broadcasted_iota(jnp.int32, grid_ref.shape, 0) - HALO).astype(F32).astype(BF16)


def fill_pair(op, grid_ref, links, metric, pair, first_col, all_cols):
    span = TILE + 2 * HALO
    for half in range(2):
        at = (2 * pair + half) * TILE
        cols = pl.ds(pl.multiple_of(at, TILE), TILE)
        lanes = slice(half * TILE, (half + 1) * TILE)
        fill_operator(op.at[half * TILE : half * TILE + span, lanes], grid_ref, links, metric, cols, first_col + at, all_cols)


def clear_corners(op):
    op[TILE + 2 * HALO :, :TILE] = jnp.zeros((TILE, TILE), BF16)
    op[:TILE, TILE:] = jnp.zeros((TILE, TILE), BF16)


def edge_columns(inner_ref, outer_ref, rows, paired):
    inner, outer = inner_ref[rows], outer_ref[rows]
    if not paired:
        return inner, outer
    odd = lax.rem(lax.axis_index("comp"), 2) == 1
    return jnp.where(odd, inner, outer), jnp.where(odd, outer, inner)


def diffuse_kernel(
    all_cols, paired, atm_hbm, inner_ref, outer_ref, links, metric, base_hbm, edges_hbm, atm_ref, wide_ref, base_ref,
    edges_ref, even_op, odd_op, grid_ref, in_sems, out_sems, edge_sem,
):
    levels, atm_rows, _ = atm_ref.shape
    rows, columns = base_ref.shape
    pairs = columns // (2 * TILE)
    fields = rows // levels
    top = upper_half(fields)
    first_col = lax.axis_index("comp") * columns
    parts = in_sems.shape[0]
    deep = atm_rows // parts

    def into(index):
        at = pl.ds(deep * index, deep)
        return pltpu.make_async_copy(atm_hbm.at[:, at, :], atm_ref.at[:, at, :], in_sems.at[index])

    def out_of(index):
        cols = pl.ds(pl.multiple_of(4 * TILE * index, TILE), 4 * TILE)
        return pltpu.make_async_copy(base_ref.at[:, cols], base_hbm.at[:, cols], out_sems.at[index])

    for index in range(parts):
        into(index).start()
    edges_ref[0], edges_ref[1] = edge_columns(inner_ref, outer_ref, slice(rows, None), paired)
    edges = pltpu.make_async_copy(edges_ref, edges_hbm, edge_sem)
    edges.start()
    place_grid(grid_ref)
    for op in (even_op, odd_op):
        clear_corners(op)
    wide_ref[:, :HALO], wide_ref[:, HALO + columns :] = edge_columns(inner_ref, outer_ref, slice(0, rows), paired)

    def narrow(pair):
        lands = pl.ds(pl.multiple_of(pair * 2 * TILE + HALO, TILE), 2 * TILE)
        both = halves(atm_ref, pl.multiple_of(8 * pair, 8), top)
        wide_ref[:, lands] = jnp.concatenate(both, axis=1).astype(BF16)

    def step(pair, op, next_op, ahead):
        at = pl.multiple_of(pair * 2 * TILE, 2 * TILE)
        done = jnp.dot(wide_ref[:, pl.ds(at, 2 * TILE + 2 * HALO)], op[...], preferred_element_type=F32)
        if next_op is not None:
            fill_pair(next_op, grid_ref, links, metric, pair + 1, first_col, all_cols)
        if ahead:
            narrow(pair + 2)
        base_ref[:, pl.ds(at, 2 * TILE)] = done.astype(BF16)

    fill_pair(even_op, grid_ref, links, metric, 0, first_col, all_cols)
    into(0).wait()
    narrow(0)
    narrow(1)

    def two_pairs(index, carry):
        step(2 * index, even_op, odd_op, True)
        step(2 * index + 1, odd_op, even_op, True)
        out_of(index).start()
        return carry

    for part in range(parts):
        last = part == parts - 1
        if not last:
            into(part + 1).wait()
        per = pairs // 2 // parts
        lax.fori_loop(part * per, (part + 1) * per - last, two_pairs, 0)
    step(pairs - 2, even_op, odd_op, False)
    step(pairs - 1, odd_op, None, False)
    out_of(pairs // 2 - 1).start()
    for index in range(pairs // 2):
        out_of(index).wait()
    edges.wait()


def diffusion(all_cols, paired, atm_rows, inner, outer, links, metric):
    levels, count, _ = atm_rows.shape
    columns = links.shape[1]
    rows = levels * count // (columns // TILE)
    edges = (2, inner.shape[0] - rows, HALO)
    return pl.pallas_call(
        functools.partial(diffuse_kernel, all_cols, paired),
        out_shape=(pltpu.HBM((rows, columns), BF16), pltpu.HBM(edges, BF16)),
        in_specs=[in_hbm()] + [in_vmem()] * 4,
        out_specs=(in_hbm(),) * 2,
        scratch_shapes=[
            pltpu.VMEM(atm_rows.shape, F32),
            pltpu.VMEM((rows, columns + 2 * HALO), BF16),
            pltpu.VMEM((rows, columns), BF16),
            pltpu.VMEM(edges, BF16),
            pltpu.VMEM((2 * (TILE + HALO), 2 * TILE), BF16),
            pltpu.VMEM((2 * (TILE + HALO), 2 * TILE), BF16),
            pltpu.VMEM((TILE + 2 * HALO, TILE), BF16),
            pltpu.SemaphoreType.DMA((4,)),
            pltpu.SemaphoreType.DMA((columns // (4 * TILE),)),
            pltpu.SemaphoreType.DMA,
        ],
        compiler_params=limit(12),
        name="diffusion",
    )(outside(atm_rows), inner, outer, links, metric)


def spread_kernel(blocks, source_ref, returned_ref, select_ref, weight_ref, out_ref, row_ref):
    tiles = weight_ref.shape[0]
    both = out_ref.shape[1]
    devs, per, _ = returned_ref.shape
    stack = returned_ref[...].reshape(devs * per, TILE)
    row_ref[...] = jnp.dot(select_ref[...], stack, preferred_element_type=F32)
    out_ref[...] = jnp.zeros_like(out_ref)
    for tile in range(tiles):
        block = lax.rem(source_ref[tile], blocks)
        back = lax.dot_general(
            row_ref[both * tile : both * (tile + 1)].astype(BF16),
            weight_ref[tile],
            (((1,), (1,)), ((), ())),
            preferred_element_type=F32,
        )
        out_ref[block] += back


def spreading(returned, tile_source, tile_weights, select, blocks, fields):
    tiles = tile_weights.shape[0]
    return pl.pallas_call(
        functools.partial(spread_kernel, blocks),
        out_shape=jax.ShapeDtypeStruct((blocks, 2 * fields, TILE), F32),
        in_specs=[in_smem()] + [in_vmem()] * 3,
        out_specs=in_vmem(),
        scratch_shapes=[pltpu.VMEM((tiles * 2 * fields, TILE), F32)],
        compiler_params=limit(8),
        name="spreading",
    )(tile_source, returned, select, tile_weights)


def update_kernel(
    all_cols, atm_w, ocn_w, atm_base, ocn_hbm, edges_ref, ocn_links, ocn_metric, own_ref, other_ref,
    atm_out, ocn_out, ocn_wide, even_op, odd_op, grid_ref, ocn_ref, atm_new, ocn_new,
    in_sems, sems,
):
    levels, atm_rows, _ = atm_new.shape
    fields, ocn_levels, columns = ocn_ref.shape
    pairs = columns // (2 * TILE)
    top = upper_half(fields)
    comp = lax.axis_index("comp")

    def into(index):
        cols = pl.ds(pl.multiple_of(4 * TILE * index, TILE), 4 * TILE)
        return pltpu.make_async_copy(ocn_hbm.at[:, :, cols], ocn_ref.at[:, :, cols], in_sems.at[index])

    for index in range(pairs // 2):
        into(index).start()
    ocn_wide[:, :HALO] = edges_ref[0]
    ocn_wide[:, HALO + columns :] = edges_ref[1]
    for op in (even_op, odd_op):
        clear_corners(op)
    place_grid(grid_ref)

    def narrow(pair):
        at = pl.multiple_of(pair * 2 * TILE, 2 * TILE)
        lands = pl.ds(pl.multiple_of(at + HALO, TILE), 2 * TILE)
        ocn_wide[:, lands] = jnp.concatenate(
            [ocn_ref[field, :, pl.ds(at, 2 * TILE)] for field in range(fields)], axis=0
        ).astype(BF16)

    def fill(pair, op):
        fill_pair(op, grid_ref, ocn_links, ocn_metric, pair, comp * columns, all_cols)

    def gains(pair):
        return [flux_gain * (own_ref[2 * pair + half] + other_ref[2 * pair + half]) for half in range(2)]

    def atm_step(index):
        for pair in (2 * index, 2 * index + 1):
            flux = gains(pair)
            base = atm_base[:, pl.ds(pl.multiple_of(pair * 2 * TILE, 2 * TILE), 2 * TILE)].astype(F32)
            gain = jnp.concatenate([flux[0][:fields], flux[1][:fields]], axis=0)
            rows = pl.ds(pl.multiple_of(8 * pair, 8), 8)
            for level in range(0, levels, 2):
                here = base[level * fields : level * fields + 8]
                low = jnp.where(top, here[:, :TILE], turned(here[:, TILE:]))
                high = jnp.where(top, turned(here[:, :TILE]), here[:, TILE:])
                atm_new[level, rows, :] = low + atm_w[level : level + 1] * gain
                atm_new[level + 1, rows, :] = high + atm_w[level + 1 : level + 2] * gain
        atm_out_of(index).start()

    def ocn_step(pair, op, next_op, ahead):
        at = pl.multiple_of(pair * 2 * TILE, 2 * TILE)
        flux = gains(pair)
        done = jnp.dot(ocn_wide[:, pl.ds(at, 2 * TILE + 2 * HALO)], op[...], preferred_element_type=F32)
        if next_op is not None:
            fill(pair + 1, next_op)
        if ahead:
            narrow(pair + 2)
        for half in range(2):
            cols = pl.ds(pl.multiple_of(at + half * TILE, TILE), TILE)
            part = slice(half * TILE, (half + 1) * TILE)
            for field in range(fields):
                ocn_new[field, :, cols] = (
                    done[field * ocn_levels : (field + 1) * ocn_levels, part]
                    + ocn_w[...] * flux[half][fields + field : fields + field + 1]
                )

    def atm_out_of(index):
        rows = pl.ds(pl.multiple_of(16 * index, 16), 16)
        return pltpu.make_async_copy(atm_new.at[:, rows, :], atm_out.at[:, rows, :], sems.at[index, 0])

    def ocn_out_of(index):
        cols = pl.ds(pl.multiple_of(4 * TILE * index, TILE), 4 * TILE)
        return pltpu.make_async_copy(ocn_new.at[:, :, cols], ocn_out.at[:, :, cols], sems.at[index, 1])

    twos = pairs // 2
    lead = min(2, twos)
    for index in range(lead):
        atm_step(index)
    fill(0, even_op)
    into(0).wait()
    narrow(0)
    narrow(1)

    def two_pairs(index, carry):
        into(index + 1).wait()
        ocn_step(2 * index, even_op, odd_op, True)
        ocn_step(2 * index + 1, odd_op, even_op, True)
        ocn_out_of(index).start()

        @pl.when(index + lead < twos)
        def _():
            atm_step(index + lead)

        return carry

    lax.fori_loop(0, twos - 1, two_pairs, 0)
    ocn_step(pairs - 2, even_op, odd_op, False)
    ocn_step(pairs - 1, odd_op, None, False)
    ocn_out_of(twos - 1).start()
    for index in range(twos):
        atm_out_of(index).wait()
        ocn_out_of(index).wait()


def update(
    all_cols, atm_wide, ocn_wide, atm_base, ocn_state, edges, ocn_links, ocn_metric, own, other
):
    fields, ocn_levels, columns = ocn_state.shape
    atm_shape = (atm_wide.shape[0], columns // TILE * fields, TILE)
    return pl.pallas_call(
        functools.partial(update_kernel, all_cols),
        out_shape=(pltpu.HBM(atm_shape, F32), pltpu.HBM(ocn_state.shape, F32)),
        in_specs=[in_vmem()] * 3 + [in_hbm()] + [in_vmem()] * 5,
        out_specs=(in_hbm(),) * 2,
        scratch_shapes=[
            pltpu.VMEM((fields * ocn_levels, columns + 2 * HALO), BF16),
            pltpu.VMEM((2 * (TILE + HALO), 2 * TILE), BF16),
            pltpu.VMEM((2 * (TILE + HALO), 2 * TILE), BF16),
            pltpu.VMEM((TILE + 2 * HALO, TILE), BF16),
            pltpu.VMEM(ocn_state.shape, F32),
            pltpu.VMEM(atm_shape, F32),
            pltpu.VMEM(ocn_state.shape, F32),
            pltpu.SemaphoreType.DMA((columns // (4 * TILE),)),
            pltpu.SemaphoreType.DMA((columns // (4 * TILE), 2)),
        ],
        compiler_params=limit(20),
        name="update",
    )(atm_wide, ocn_wide, atm_base, outside(ocn_state), edges, ocn_links, ocn_metric, own, other)


def exchanged(inner, outer, axis):
    count = lax.axis_size(axis)
    if count % 2:
        onward = [(i, (i + 1) % count) for i in range(count)]
        return lax.ppermute(inner, axis, onward), lax.ppermute(outer, axis, [(j, i) for i, j in onward])
    within = [(i, i ^ 1) for i in range(count)]
    across = [(i, (i - 1 if i % 2 == 0 else i + 1) % count) for i in range(count)]
    return lax.ppermute(inner, axis, within), lax.ppermute(outer, axis, across)


def routes(tile_source, tile_target, owner_map, blocks, fields, dev_count):
    tiles = tile_source.shape[0]
    xblocks = owner_map.shape[0]
    per = fields * CAP
    matched = tile_target[:, None] == jnp.arange(xblocks, dtype=jnp.int32)[None, :]
    placed_at = jnp.sum(jnp.where(matched, owner_map[None, :], 0), axis=1)
    owner = placed_at // XB_DEV
    side = (tile_source >= blocks).astype(jnp.int32)
    segment = side * XB_DEV + placed_at % XB_DEV
    index = jnp.arange(tiles, dtype=jnp.int32)
    before = (index[None, :] < index[:, None]) & (owner[None, :] == owner[:, None])
    rank = jnp.sum(before.astype(jnp.int32), axis=1)
    slots = jnp.arange(dev_count * 8, dtype=jnp.int32)
    at_slot = (slots[:, None] // 8 == owner[None, :]) & (slots[:, None] % CAP == rank[None, :])
    label = jnp.sum(jnp.where(at_slot, segment[None, :] + 1, 0), axis=1) - 1
    labels = jnp.broadcast_to(label.astype(F32)[:, None], (dev_count * 8, TILE)).reshape(dev_count, 8, TILE)
    column = jnp.arange(tiles * 2 * fields, dtype=jnp.int32)
    mine = column[:, None] // (2 * fields) == index[None, :]
    packed = jnp.sum(jnp.where(mine, (2 * (owner * per + rank) + side)[None, :], 0), axis=1)
    goes = jnp.where(
        packed % 2 == column // fields % 2, packed // 2 + column % fields * CAP, -1
    )
    rows = jnp.arange(dev_count * per, dtype=jnp.int32)
    to_slots = (rows[:, None] == goes[None, :]).astype(BF16)
    to_tiles = (goes[:, None] == rows[None, :]).astype(BF16)
    return labels, to_slots, to_tiles


def shards(
    atm_state,
    ocn_state,
    atm_weights,
    ocn_weights,
    atm_metric,
    ocn_metric,
    atm_links,
    ocn_links,
    tile_weights,
    tile_source,
    tile_target,
    owner_map,
):
    comp_count = lax.axis_size("comp")
    dev_count = comp_count * lax.axis_size("lev")
    fields, _, columns = atm_state.shape
    blocks = columns // TILE
    swap = [(0, 1), (1, 0)]

    paired = comp_count % 2 == 0
    part, inner, outer, atm_wide, ocn_wide = surface(
        to_rows(atm_state), ocn_state, atm_weights, ocn_weights, paired
    )
    part_other = lax.ppermute(part, "lev", swap)
    labels, to_slots, to_tiles = routes(tile_source, tile_target, owner_map, blocks, fields, dev_count)
    outgoing = contributions(part, part_other, tile_source, tile_weights, to_slots, labels)
    outgoing, inner, outer = lax.optimization_barrier((outgoing, inner, outer))
    arrived = lax.all_to_all(outgoing, BOTH, split_axis=0, concat_axis=0, tiled=True)
    inner, outer = exchanged(inner, outer, "comp")
    xgrid, answer = fluxes(arrived, fields)
    answer, links = lax.optimization_barrier((answer, atm_links))
    returned = lax.all_to_all(answer, BOTH, split_axis=0, concat_axis=0, tiled=True)
    all_cols = columns * comp_count
    atm_base, edges = diffusion(all_cols, paired, to_rows(atm_state), inner, outer, links, atm_metric)
    returned, atm_base, edges = lax.optimization_barrier((returned, atm_base, edges))
    spread = spreading(returned, tile_source, tile_weights, to_tiles, blocks, fields)
    spread_other = lax.ppermute(spread, "lev", swap)
    atm_new, ocn_new = update(
        all_cols, atm_wide, ocn_wide, atm_base, ocn_state, edges, ocn_links, ocn_metric, spread, spread_other
    )
    return (from_rows(atm_new, fields), ocn_new, xgrid)


def solution(mesh):
    placed = (
        P(None, "lev", ("grp", "comp")),
        P(None, "lev", ("grp", "comp")),
        P("lev"),
        P("lev"),
        P(None, "comp"),
        P(None, "comp"),
        P(None, "comp"),
        P(None, "comp"),
        P(("comp", "lev"), None, None),
        P(("comp", "lev")),
        P(("comp", "lev")),
        P(),
    )
    return jax.shard_map(
        shards,
        mesh=mesh,
        in_specs=placed,
        out_specs=(
            P(None, "lev", ("grp", "comp")),
            P(None, "lev", ("grp", "comp")),
            P(("grp", "comp", "lev"), None, None),
        ),
        check_vma=False,
    )
```

time: 50.8 us -> 44.9 us (0.88)
  Pallas kernels: 24.2 us -> 19.8 us
  waiting for transfers between devices: 8.17 us -> 5.68 us
  starting transfers between devices: 15.9 us -> 17.2 us
    all_to_all x1, waiting for transfers between devices: 6.07 us -> 1.57 us  [shards(): lax.all_to_all(answer, BOTH, split_axis=0, concat_axis=0, tiled=True)]
    pallas_call x4, Pallas kernels: 21.1 us -> 16.7 us  [the longest x1 6.39 us: update(): pl.pallas_call(functools.partial(update_kernel, all_cols), out_shape=(plt...]
    all_to_all x1, waiting for transfers between devices: 0.01 us -> 2.58 us  [shards(): lax.all_to_all(outgoing, BOTH, split_axis=0, concat_axis=0, tiled=True)]
    ppermute x2, waiting for transfers between devices: 0.76 us -> 0.01 us  [the longest x1 0.01 us: exchanged(): lax.ppermute(inner, axis, within)]
    all_to_all x1, starting transfers between devices: 3.51 us -> 4.15 us  [shards(): lax.all_to_all(answer, BOTH, split_axis=0, concat_axis=0, tiled=True)]
  transfers between devices with their start and end apart: 6 -> 6, of which waited for: 3 -> 4; matrix products, arithmetic and copies ran while one was open for 2% -> 2% of each run, Pallas kernels for 22% -> 14%
where the time goes in v2:
time: 44.9 us; the launch traced here: 44.6 us
  Pallas kernels  19.8 us (44%)
  starting transfers between devices  17.2 us (38%)
  waiting for transfers between devices  5.68 us (13%)
  between operations  0.86 us (2%)
  other arithmetic  0.79 us (2%)
    all_to_all x1, starting transfers between devices, shards(): lax.all_to_all(outgoing, BOTH, split_axis=0, concat_axis=0, tiled=True)  7.29 us
    pallas_call x1, Pallas kernels, update(): pl.pallas_call(functools.partial(update_kernel, all_cols), out_shape=(plt...  6.39 us
    pallas_call x1, Pallas kernels, diffusion(): pl.pallas_call(functools.partial(diffuse_kernel, all_cols, paired), out_s...  5.13 us
    all_to_all x1, starting transfers between devices, shards(): lax.all_to_all(answer, BOTH, split_axis=0, concat_axis=0, tiled=True)  4.15 us
    ppermute x1, starting transfers between devices, exchanged(): lax.ppermute(outer, axis, across)  3.27 us
    pallas_call x1, Pallas kernels, surface(): pl.pallas_call(functools.partial(surface_kernel, chunks, paired), out_sha...  2.95 us
    all_to_all x1, waiting for transfers between devices, shards(): lax.all_to_all(outgoing, BOTH, split_axis=0, concat_axis=0, tiled=True)  2.58 us
    pallas_call x1, Pallas kernels, spreading(): pl.pallas_call(functools.partial(spread_kernel, blocks), out_shape=jax.Sh...  2.27 us
  transfers between devices with their start and end apart: 6, of which 4 were waited for; matrix products, arithmetic and copies ran while one was open for 2% of the time, Pallas kernels for 14%

profile of v2, /device:TPU:0, one launch (start us, length us, event | category | flops | bytes accessed | tf_op | source)
XLA Modules:
  0.0 44.6 jit_solution(14631731155760975067)
XLA Ops:
  0.6 0.0 copy-start.10
  0.6 0.0 copy-start.11
  0.7 0.0 copy-start.9
  0.7 0.0 copy-start
  0.7 3.0 %surface.1 = (f32[32,8,128]{2,1,0:T(8,128)S(1)}, bf16[304,128]{1,0:T(8,128)(2,1)S(1)}, bf16[304,128]{1,0:T(8,128)(2,1)S(1)}, f32[36,128]{1,0:T(8,128)}, f32[40,128]{1,0:T(8,128)}) custom-call(f32[36,128,128]{2,1,0:T(8,128)} %bitcast.14, f32[4,40,4096]{2,1,0:T(8,128)} %ocn_hbm.3, f32[36]{0:T(128)} %atm_w.1, f32[40]{0:T(128)} %ocn_w.1), custom_call_target="tpu_custom_call" | custom-call | tf_op jit(solution)/shard_map/surface/pallas_call | solution.py:153
  3.6 0.0 copy-start.5
  3.6 0.0 copy-start.6
  3.7 0.5 %collective-permute-start = (f32[32,8,128]{2,1,0:T(8,128)S(1)}, f32[32,8,128]{2,1,0:T(8,128)S(1)}, u32[]{:S(2)}, u32[]{:S(2)}) collective-permute-start(f32[32,8,128]{2,1,0:T(8,128)S(1)} %get-tuple-element.24.own_ref), channel_id=1, source_target_pairs={{0,1},{1,0},{2,3},{3,2},{4,5},{5,4},{6,7},{7,6},{8,9},{9,8},{10,11... | collective-permute-start | bytes 393224 | tf_op jit(solution)/shard_map/ppermute | solution.py:648
  4.2 0.0 copy-done.10
  4.2 0.0 copy-done.11
  4.2 0.2 select_reduce_fusion.1
  4.4 0.0 copy-done.9
  4.4 0.2 convert_reduce_fusion
  4.6 0.1 select_reduce_fusion.2
  4.7 0.1 select_reduce_fusion
  4.8 0.1 convert_element_type.26
  4.9 0.1 fusion.select_ref
  5.0 0.2 collective-permute-done.other_ref
  5.2 0.1 broadcast_in_dim.46.label_ref
  5.2 0.0 copy-done
  5.2 2.0 %contributions.1 = bf16[16,24,128]{2,1,0:T(8,128)(2,1)} custom-call(s32[64]{0:T(128)S(1)} %copy-done.9, f32[32,8,128]{2,1,0:T(8,128)S(1)} %get-tuple-element.24.own_ref, f32[32,8,128]{2,1,0:T(8,128)S(1)} %collective-permute-done.other_ref, bf16[64,128,128]{2,1,0:T(8,128)(2,1)S(1)} %copy-done, bf16[256,512]{1,0:T(8,128)(2,1)S(1)} %fusion.select_ref, ...), custom_call_target="tpu_custom_call" | custom-call | tf_op jit(solution)/shard_map/contributions/pallas_call | solution.py:203
  7.3 7.3 %all-to-all-start = ((bf16[16,24,128]{2,1,0:T(8,128)(2,1)}), bf16[16,24,128]{2,1,0:T(8,128)(2,1)S(1)}, u32[]{:S(2)}, u32[]{:S(2)}) async-start(bf16[16,24,128]{2,1,0:T(8,128)(2,1)} %contributions.1), calls=%async_computation | async-start | bytes 196608 | tf_op jit(solution)/shard_map/all_to_all | solution.py:652
  14.6 1.9 %collective-permute-start.1 = (bf16[304,128]{1,0:T(8,128)(2,1)S(1)}, bf16[304,128]{1,0:T(8,128)(2,1)S(1)}, u32[]{:S(2)}, u32[]{:S(2)}) collective-permute-start(bf16[304,128]{1,0:T(8,128)(2,1)S(1)} %get-tuple-element.30), channel_id=1, source_target_pairs={{0,2},{2,0},{4,6},{6,4},{8,10},{10,8},{12,14},{14,12},{1,3},{3,1},... | collective-permute-start | bytes 233480 | tf_op jit(solution)/shard_map/ppermute | solution.py:593
  16.5 3.3 %collective-permute-start.2 = (bf16[304,128]{1,0:T(8,128)(2,1)S(1)}, bf16[304,128]{1,0:T(8,128)(2,1)S(1)}, u32[]{:S(2)}, u32[]{:S(2)}) collective-permute-start(bf16[304,128]{1,0:T(8,128)(2,1)S(1)} %get-tuple-element.31), channel_id=1, source_target_pairs={{0,14},{2,4},{4,2},{6,8},{8,6},{10,12},{12,10},{14,0},{1,15},{3,5}... | collective-permute-start | bytes 233480 | tf_op jit(solution)/shard_map/ppermute | solution.py:593
  19.8 2.6 %all-to-all-done.arrived_ref = bf16[16,24,128]{2,1,0:T(8,128)(2,1)S(1)} async-done(((bf16[16,24,128]{2,1,0:T(8,128)(2,1)}), bf16[16,24,128]{2,1,0:T(8,128)(2,1)S(1)}, u32[]{:S(2)}, u32[]{:S(2)}) %all-to-all-start) | async-done | bytes 98336 | tf_op jit(solution)/shard_map/all_to_all | solution.py:652
  22.4 1.1 %fluxes.1 = (bf16[16,8,128]{2,1,0:T(8,128)(2,1)}, bf16[16,16,128]{2,1,0:T(8,128)(2,1)}) custom-call(bf16[16,24,128]{2,1,0:T(8,128)(2,1)S(1)} %all-to-all-done.arrived_ref), custom_call_target="tpu_custom_call" | custom-call | tf_op jit(solution)/shard_map/fluxes/pallas_call | solution.py:258
  23.4 4.1 %all-to-all-start.1 = ((bf16[16,16,128]{2,1,0:T(8,128)(2,1)}), bf16[16,16,128]{2,1,0:T(8,128)(2,1)}, u32[]{:S(2)}, u32[]{:S(2)}) async-start(bf16[16,16,128]{2,1,0:T(8,128)(2,1)} %get-tuple-element.29), calls=%async_computation.1 | async-start | bytes 131072 | tf_op jit(solution)/shard_map/all_to_all | solution.py:656
  27.6 0.1 fusion.1.select_ref
  27.7 0.0 collective-permute-done.1.inner_ref
  27.7 0.0 collective-permute-done.2.outer_ref
  27.7 0.0 copy-done.5
  27.7 0.0 copy-done.6
  27.7 5.1 %diffusion.1 = (bf16[144,4096]{1,0:T(8,128)(2,1)}, bf16[2,160,128]{2,1,0:T(8,128)(2,1)}) custom-call(f32[36,128,128]{2,1,0:T(8,128)} %bitcast.15, bf16[304,128]{1,0:T(8,128)(2,1)S(1)} %collective-permute-done.1.inner_ref, bf16[304,128]{1,0:T(8,128)(2,1)S(1)} %collective-permute-done.2.outer_ref, s32[4,4096]{1,0:T(4,128)S(1)} %copy-done.5, ...), custom_call_target="tpu_custom_call" | custom-call | tf_op jit(solution)/shard_map/diffusion/pallas_call | solution.py:402
  32.9 0.0 copy-start.1
  32.9 1.6 %all-to-all-done.1.returned_ref = bf16[16,16,128]{2,1,0:T(8,128)(2,1)} async-done(((bf16[16,16,128]{2,1,0:T(8,128)(2,1)}), bf16[16,16,128]{2,1,0:T(8,128)(2,1)}, u32[]{:S(2)}, u32[]{:S(2)}) %all-to-all-start.1) | async-done | bytes 65568 | tf_op jit(solution)/shard_map/all_to_all | solution.py:656
  34.5 0.0 copy-start.2
  34.5 0.0 copy-start.4
  34.5 0.0 copy-start.8
  34.5 2.3 %spreading.1.own_ref = f32[32,8,128]{2,1,0:T(8,128)S(1)} custom-call(s32[64]{0:T(128)S(1)} %copy-done.9, bf16[16,16,128]{2,1,0:T(8,128)(2,1)} %all-to-all-done.1.returned_ref, bf16[512,256]{1,0:T(8,128)(2,1)S(1)} %fusion.1.select_ref, bf16[64,128,128]{2,1,0:T(8,128)(2,1)S(1)} %copy-done), custom_call_target="tpu_custom_call" | custom-call | tf_op jit(solution)/shard_map/spreading/pallas_call | solution.py:444
  36.8 0.0 collective-permute-start.3
  36.8 1.3 %collective-permute-done.3.other_ref = f32[32,8,128]{2,1,0:T(8,128)S(1)} collective-permute-done((f32[32,8,128]{2,1,0:T(8,128)S(1)}, f32[32,8,128]{2,1,0:T(8,128)S(1)}, u32[]{:S(2)}, u32[]{:S(2)}) %collective-permute-start.3) | collective-permute-done | bytes 131104 | tf_op jit(solution)/shard_map/ppermute | solution.py:661
  38.1 0.0 copy-done.1
  38.1 0.0 copy-done.2
  38.1 0.0 copy-done.3
  38.1 0.0 copy-done.4
  38.2 0.0 copy-done.7
  38.2 0.0 copy-done.8
  38.2 6.4 %update.1 = (f32[36,128,128]{2,1,0:T(8,128)}, f32[4,40,4096]{2,1,0:T(8,128)}) custom-call(f32[36,128]{1,0:T(8,128)S(1)} %copy-done.7, f32[40,128]{1,0:T(8,128)S(1)} %copy-done.8, bf16[144,4096]{1,0:T(8,128)(2,1)S(1)} %copy-done.1, f32[4,40,4096]{2,1,0:T(8,128)} %ocn_hbm.3, bf16[2,160,128]{2,1,0:T(8,128)(2,1)S(1)} %copy-done.4, s32[6,4096]{1,0:T(8,128)S(1)} %copy-done.2, ...), custom_call_target="tpu_custom_call" | custom-call | tf_op jit(solution)/shard_map/update/pallas_call | solution.py:565
  (8 shorter events, 0.1 us)
Async XLA Ops:
  0.6 3.6 %copy-start.10 = (s32[256]{0:T(256)S(1)}, s32[256]{0:T(256)}, u32[]{:S(2)}) copy-start(s32[256]{0:T(256)} %param.23) | copy-start | bytes 3076
  0.6 3.5 %copy-start.11 = (s32[64]{0:T(128)S(1)}, s32[64]{0:T(128)}, u32[]{:S(2)}) copy-start(s32[64]{0:T(128)} %param.22) | copy-start | bytes 772
  0.7 3.7 %copy-start.9 = (s32[64]{0:T(128)S(1)}, s32[64]{0:T(128)}, u32[]{:S(2)}) copy-start(s32[64]{0:T(128)} %source_ref.3) | copy-start | bytes 772
  0.7 4.6 %copy-start = (bf16[64,128,128]{2,1,0:T(8,128)(2,1)S(1)}, bf16[64,128,128]{2,1,0:T(8,128)(2,1)}, u32[]{:S(2)}) copy-start(bf16[64,128,128]{2,1,0:T(8,128)(2,1)} %weight_ref.3) | copy-start | bytes 6291460
  3.6 24.1 %copy-start.5 = (s32[4,4096]{1,0:T(4,128)S(1)}, s32[4,4096]{1,0:T(4,128)}, u32[]{:S(2)}) copy-start(s32[4,4096]{1,0:T(4,128)} %links) | copy-start | bytes 196612
  3.6 24.1 %copy-start.6 = (f32[4,4096]{1,0:T(4,128)S(1)}, f32[4,4096]{1,0:T(4,128)}, u32[]{:S(2)}) copy-start(f32[4,4096]{1,0:T(4,128)} %metric.1) | copy-start | bytes 196612
  3.7 1.5 %collective-permute-start = (f32[32,8,128]{2,1,0:T(8,128)S(1)}, f32[32,8,128]{2,1,0:T(8,128)S(1)}, u32[]{:S(2)}, u32[]{:S(2)}) collective-permute-start(f32[32,8,128]{2,1,0:T(8,128)S(1)} %get-tuple-element.24.own_ref), channel_id=1, source_target_pairs={{0,1},{1,0},{2,3},{3,2},{4,5},{5,4},{6,7},{7,6},{8,9},{9,8},{10,11... | collective-permute-start | bytes 393224 | tf_op jit(solution)/shard_map/ppermute | solution.py:648
  7.3 15.1 %all-to-all-start = ((bf16[16,24,128]{2,1,0:T(8,128)(2,1)}), bf16[16,24,128]{2,1,0:T(8,128)(2,1)S(1)}, u32[]{:S(2)}, u32[]{:S(2)}) async-start(bf16[16,24,128]{2,1,0:T(8,128)(2,1)} %contributions.1), calls=%async_computation | async-start | bytes 196608 | tf_op jit(solution)/shard_map/all_to_all | solution.py:652
  14.6 13.1 %collective-permute-start.1 = (bf16[304,128]{1,0:T(8,128)(2,1)S(1)}, bf16[304,128]{1,0:T(8,128)(2,1)S(1)}, u32[]{:S(2)}, u32[]{:S(2)}) collective-permute-start(bf16[304,128]{1,0:T(8,128)(2,1)S(1)} %get-tuple-element.30), channel_id=1, source_target_pairs={{0,2},{2,0},{4,6},{6,4},{8,10},{10,8},{12,14},{14,12},{1,3},{3,1},... | collective-permute-start | bytes 233480 | tf_op jit(solution)/shard_map/ppermute | solution.py:593
  16.5 11.2 %collective-permute-start.2 = (bf16[304,128]{1,0:T(8,128)(2,1)S(1)}, bf16[304,128]{1,0:T(8,128)(2,1)S(1)}, u32[]{:S(2)}, u32[]{:S(2)}) collective-permute-start(bf16[304,128]{1,0:T(8,128)(2,1)S(1)} %get-tuple-element.31), channel_id=1, source_target_pairs={{0,14},{2,4},{4,2},{6,8},{8,6},{10,12},{12,10},{14,0},{1,15},{3,5}... | collective-permute-start | bytes 233480 | tf_op jit(solution)/shard_map/ppermute | solution.py:593
  23.4 11.1 %all-to-all-start.1 = ((bf16[16,16,128]{2,1,0:T(8,128)(2,1)}), bf16[16,16,128]{2,1,0:T(8,128)(2,1)}, u32[]{:S(2)}, u32[]{:S(2)}) async-start(bf16[16,16,128]{2,1,0:T(8,128)(2,1)} %get-tuple-element.29), calls=%async_computation.1 | async-start | bytes 131072 | tf_op jit(solution)/shard_map/all_to_all | solution.py:656
  32.9 5.2 %copy-start.1 = (bf16[144,4096]{1,0:T(8,128)(2,1)S(1)}, bf16[144,4096]{1,0:T(8,128)(2,1)}, u32[]{:S(2)}) copy-start(bf16[144,4096]{1,0:T(8,128)(2,1)} %get-tuple-element.35.atm_base) | copy-start | bytes 3538948
  34.5 3.7 %copy-start.2 = (s32[6,4096]{1,0:T(8,128)S(1)}, s32[6,4096]{1,0:T(8,128)}, u32[]{:S(2)}) copy-start(s32[6,4096]{1,0:T(8,128)} %ocn_links.1) | copy-start | bytes 294916
  34.5 3.7 %copy-start.3 = (f32[6,4096]{1,0:T(8,128)S(1)}, f32[6,4096]{1,0:T(8,128)}, u32[]{:S(2)}) copy-start(f32[6,4096]{1,0:T(8,128)} %ocn_metric.1) | copy-start | bytes 294916
  34.5 3.7 %copy-start.4 = (bf16[2,160,128]{2,1,0:T(8,128)(2,1)S(1)}, bf16[2,160,128]{2,1,0:T(8,128)(2,1)}, u32[]{:S(2)}) copy-start(bf16[2,160,128]{2,1,0:T(8,128)(2,1)} %get-tuple-element.36.edges_ref) | copy-start | bytes 245764
  34.5 3.7 %copy-start.7 = (f32[36,128]{1,0:T(8,128)S(1)}, f32[36,128]{1,0:T(8,128)}, u32[]{:S(2)}) copy-start(f32[36,128]{1,0:T(8,128)} %get-tuple-element.22.atm_w) | copy-start | bytes 55300
  34.5 3.7 %copy-start.8 = (f32[40,128]{1,0:T(8,128)S(1)}, f32[40,128]{1,0:T(8,128)}, u32[]{:S(2)}) copy-start(f32[40,128]{1,0:T(8,128)} %get-tuple-element.23.ocn_w) | copy-start | bytes 61444
  36.8 1.4 %collective-permute-start.3 = (f32[32,8,128]{2,1,0:T(8,128)S(1)}, f32[32,8,128]{2,1,0:T(8,128)S(1)}, u32[]{:S(2)}, u32[]{:S(2)}) collective-permute-start(f32[32,8,128]{2,1,0:T(8,128)S(1)} %spreading.1.own_ref), channel_id=1, source_target_pairs={{0,1},{1,0},{2,3},{3,2},{4,5},{5,4},{6,7},{7,6},{8,9},{9,8},{10,11... | collective-permute-start | bytes 393224 | tf_op jit(solution)/shard_map/ppermute | solution.py:661

commit v3 on v2

--- a/solution.py
+++ b/solution.py
@@ -325,21 +325,20 @@
 
 
 def diffuse_kernel(
-    all_cols, paired, atm_hbm, inner_ref, outer_ref, links, metric, base_hbm, edges_hbm, atm_ref, wide_ref, base_ref,
+    all_cols, paired, ocn_hbm, inner_ref, outer_ref, links, metric, base_hbm, edges_hbm, ocn_ref, wide_ref, base_ref,
     edges_ref, even_op, odd_op, grid_ref, in_sems, out_sems, edge_sem,
 ):
-    levels, atm_rows, _ = atm_ref.shape
-    rows, columns = base_ref.shape
+    fields, levels, columns = ocn_ref.shape
+    rows = fields * levels
+    first = inner_ref.shape[0] - rows
     pairs = columns // (2 * TILE)
-    fields = rows // levels
-    top = upper_half(fields)
     first_col = lax.axis_index("comp") * columns
     parts = in_sems.shape[0]
-    deep = atm_rows // parts
+    wide_cols = columns // parts
 
     def into(index):
-        at = pl.ds(deep * index, deep)
-        return pltpu.make_async_copy(atm_hbm.at[:, at, :], atm_ref.at[:, at, :], in_sems.at[index])
+        cols = pl.ds(wide_cols * index, wide_cols)
+        return pltpu.make_async_copy(ocn_hbm.at[:, :, cols], ocn_ref.at[:, :, cols], in_sems.at[index])
 
     def out_of(index):
         cols = pl.ds(pl.multiple_of(4 * TILE * index, TILE), 4 * TILE)
@@ -347,18 +346,20 @@
 
     for index in range(parts):
         into(index).start()
-    edges_ref[0], edges_ref[1] = edge_columns(inner_ref, outer_ref, slice(rows, None), paired)
+    edges_ref[0], edges_ref[1] = edge_columns(inner_ref, outer_ref, slice(0, first), paired)
     edges = pltpu.make_async_copy(edges_ref, edges_hbm, edge_sem)
     edges.start()
     place_grid(grid_ref)
     for op in (even_op, odd_op):
         clear_corners(op)
-    wide_ref[:, :HALO], wide_ref[:, HALO + columns :] = edge_columns(inner_ref, outer_ref, slice(0, rows), paired)
+    wide_ref[:, :HALO], wide_ref[:, HALO + columns :] = edge_columns(inner_ref, outer_ref, slice(first, None), paired)
 
     def narrow(pair):
-        lands = pl.ds(pl.multiple_of(pair * 2 * TILE + HALO, TILE), 2 * TILE)
-        both = halves(atm_ref, pl.multiple_of(8 * pair, 8), top)
-        wide_ref[:, lands] = jnp.concatenate(both, axis=1).astype(BF16)
+        at = pl.multiple_of(pair * 2 * TILE, 2 * TILE)
+        lands = pl.ds(pl.multiple_of(at + HALO, TILE), 2 * TILE)
+        wide_ref[:, lands] = jnp.concatenate(
+            [ocn_ref[field, :, pl.ds(at, 2 * TILE)] for field in range(fields)], axis=0
+        ).astype(BF16)
 
     def step(pair, op, next_op, ahead):
         at = pl.multiple_of(pair * 2 * TILE, 2 * TILE)
@@ -394,10 +395,9 @@
     edges.wait()
 
 
-def diffusion(all_cols, paired, atm_rows, inner, outer, links, metric):
-    levels, count, _ = atm_rows.shape
-    columns = links.shape[1]
-    rows = levels * count // (columns // TILE)
+def diffusion(all_cols, paired, ocn_state, inner, outer, links, metric):
+    fields, levels, columns = ocn_state.shape
+    rows = fields * levels
     edges = (2, inner.shape[0] - rows, HALO)
     return pl.pallas_call(
         functools.partial(diffuse_kernel, all_cols, paired),
@@ -405,7 +405,7 @@
         in_specs=[in_hbm()] + [in_vmem()] * 4,
         out_specs=(in_hbm(),) * 2,
         scratch_shapes=[
-            pltpu.VMEM(atm_rows.shape, F32),
+            pltpu.VMEM(ocn_state.shape, F32),
             pltpu.VMEM((rows, columns + 2 * HALO), BF16),
             pltpu.VMEM((rows, columns), BF16),
             pltpu.VMEM(edges, BF16),
@@ -418,15 +418,17 @@
         ],
         compiler_params=limit(12),
         name="diffusion",
-    )(outside(atm_rows), inner, outer, links, metric)
-
-
-def spread_kernel(blocks, source_ref, returned_ref, select_ref, weight_ref, out_ref, row_ref):
+    )(outside(ocn_state), inner, outer, links, metric)
+
+
+def spread_kernel(blocks, source_ref, returned_ref, goes_ref, weight_ref, out_ref, row_ref):
     tiles = weight_ref.shape[0]
     both = out_ref.shape[1]
     devs, per, _ = returned_ref.shape
     stack = returned_ref[...].reshape(devs * per, TILE)
-    row_ref[...] = jnp.dot(select_ref[...], stack, preferred_element_type=F32)
+    rows = lax.broadcasted_iota(jnp.int32, (devs * per, goes_ref.shape[1]), 0)
+    select = jnp.where(rows == goes_ref[...], 1.0, 0.0).astype(BF16)
+    row_ref[...] = lax.dot_general(select, stack, (((0,), (0,)), ((), ())), preferred_element_type=F32)
     out_ref[...] = jnp.zeros_like(out_ref)
     for tile in range(tiles):
         block = lax.rem(source_ref[tile], blocks)
@@ -439,7 +441,7 @@
         out_ref[block] += back
 
 
-def spreading(returned, tile_source, tile_weights, select, blocks, fields):
+def spreading(returned, tile_source, tile_weights, goes, blocks, fields):
     tiles = tile_weights.shape[0]
     return pl.pallas_call(
         functools.partial(spread_kernel, blocks),
@@ -449,138 +451,157 @@
         scratch_shapes=[pltpu.VMEM((tiles * 2 * fields, TILE), F32)],
         compiler_params=limit(8),
         name="spreading",
-    )(tile_source, returned, select, tile_weights)
+    )(tile_source, returned, goes, tile_weights)
 
 
 def update_kernel(
-    all_cols, atm_w, ocn_w, atm_base, ocn_hbm, edges_ref, ocn_links, ocn_metric, own_ref, other_ref,
-    atm_out, ocn_out, ocn_wide, even_op, odd_op, grid_ref, ocn_ref, atm_new, ocn_new,
-    in_sems, sems,
+    all_cols, atm_w_hbm, ocn_w_hbm, ocn_base, atm_hbm, edges_hbm, links_hbm, metric_hbm, own_ref, other_ref, atm_out,
+    ocn_out, atm_w, ocn_w, edges_ref, links, metric, wide_ref,
+    even_op, odd_op, grid_ref, atm_ref, atm_new, ocn_new, few_sems, in_sems, sems,
 ):
-    levels, atm_rows, _ = atm_new.shape
-    fields, ocn_levels, columns = ocn_ref.shape
+    levels, _, _ = atm_new.shape
+    fields, ocn_levels, columns = ocn_new.shape
     pairs = columns // (2 * TILE)
+    twos = pairs // 2
     top = upper_half(fields)
-    comp = lax.axis_index("comp")
+    first_col = lax.axis_index("comp") * columns
 
     def into(index):
+        rows = pl.ds(pl.multiple_of(16 * index, 16), 16)
+        return pltpu.make_async_copy(atm_hbm.at[:, rows, :], atm_ref.at[:, rows, :], in_sems.at[index])
+
+    def atm_out_of(index):
+        rows = pl.ds(pl.multiple_of(16 * index, 16), 16)
+        return pltpu.make_async_copy(atm_new.at[:, rows, :], atm_out.at[:, rows, :], sems.at[index, 0])
+
+    def ocn_out_of(index):
         cols = pl.ds(pl.multiple_of(4 * TILE * index, TILE), 4 * TILE)
-        return pltpu.make_async_copy(ocn_hbm.at[:, :, cols], ocn_ref.at[:, :, cols], in_sems.at[index])
-
-    for index in range(pairs // 2):
+        return pltpu.make_async_copy(ocn_new.at[:, :, cols], ocn_out.at[:, :, cols], sems.at[index, 1])
+
+    few = [
+        pltpu.make_async_copy(src, dst, few_sems.at[k])
+        for k, (src, dst) in enumerate(
+            (
+                (atm_w_hbm, atm_w),
+                (ocn_w_hbm, ocn_w),
+                (links_hbm, links),
+                (metric_hbm, metric),
+                (edges_hbm, edges_ref),
+            )
+        )
+    ]
+    for copy in few:
+        copy.start()
+    for index in range(twos):
         into(index).start()
-    ocn_wide[:, :HALO] = edges_ref[0]
-    ocn_wide[:, HALO + columns :] = edges_ref[1]
     for op in (even_op, odd_op):
         clear_corners(op)
     place_grid(grid_ref)
 
     def narrow(pair):
-        at = pl.multiple_of(pair * 2 * TILE, 2 * TILE)
-        lands = pl.ds(pl.multiple_of(at + HALO, TILE), 2 * TILE)
-        ocn_wide[:, lands] = jnp.concatenate(
-            [ocn_ref[field, :, pl.ds(at, 2 * TILE)] for field in range(fields)], axis=0
-        ).astype(BF16)
-
-    def fill(pair, op):
-        fill_pair(op, grid_ref, ocn_links, ocn_metric, pair, comp * columns, all_cols)
+        lands = pl.ds(pl.multiple_of(pair * 2 * TILE + HALO, TILE), 2 * TILE)
+        both = halves(atm_ref, pl.multiple_of(8 * pair, 8), top)
+        wide_ref[:, lands] = jnp.concatenate(both, axis=1).astype(BF16)
 
     def gains(pair):
         return [flux_gain * (own_ref[2 * pair + half] + other_ref[2 * pair + half]) for half in range(2)]
 
-    def atm_step(index):
+    def ocn_step(index):
         for pair in (2 * index, 2 * index + 1):
             flux = gains(pair)
-            base = atm_base[:, pl.ds(pl.multiple_of(pair * 2 * TILE, 2 * TILE), 2 * TILE)].astype(F32)
-            gain = jnp.concatenate([flux[0][:fields], flux[1][:fields]], axis=0)
-            rows = pl.ds(pl.multiple_of(8 * pair, 8), 8)
-            for level in range(0, levels, 2):
-                here = base[level * fields : level * fields + 8]
-                low = jnp.where(top, here[:, :TILE], turned(here[:, TILE:]))
-                high = jnp.where(top, turned(here[:, :TILE]), here[:, TILE:])
-                atm_new[level, rows, :] = low + atm_w[level : level + 1] * gain
-                atm_new[level + 1, rows, :] = high + atm_w[level + 1 : level + 2] * gain
-        atm_out_of(index).start()
-
-    def ocn_step(pair, op, next_op, ahead):
+            for half in range(2):
+                cols = pl.ds(pl.multiple_of((2 * pair + half) * TILE, TILE), TILE)
+                base = ocn_base[:, cols].astype(F32)
+                for field in range(fields):
+                    ocn_new[field, :, cols] = (
+                        base[field * ocn_levels : (field + 1) * ocn_levels]
+                        + ocn_w[...] * flux[half][fields + field : fields + field + 1]
+                    )
+        ocn_out_of(index).start()
+
+    def atm_step(pair, op, next_op, ahead):
         at = pl.multiple_of(pair * 2 * TILE, 2 * TILE)
         flux = gains(pair)
-        done = jnp.dot(ocn_wide[:, pl.ds(at, 2 * TILE + 2 * HALO)], op[...], preferred_element_type=F32)
+        done = jnp.dot(wide_ref[:, pl.ds(at, 2 * TILE + 2 * HALO)], op[...], preferred_element_type=F32)
         if next_op is not None:
-            fill(pair + 1, next_op)
+            fill_pair(next_op, grid_ref, links, metric, pair + 1, first_col, all_cols)
         if ahead:
             narrow(pair + 2)
-        for half in range(2):
-            cols = pl.ds(pl.multiple_of(at + half * TILE, TILE), TILE)
-            part = slice(half * TILE, (half + 1) * TILE)
-            for field in range(fields):
-                ocn_new[field, :, cols] = (
-                    done[field * ocn_levels : (field + 1) * ocn_levels, part]
-                    + ocn_w[...] * flux[half][fields + field : fields + field + 1]
-                )
-
-    def atm_out_of(index):
-        rows = pl.ds(pl.multiple_of(16 * index, 16), 16)
-        return pltpu.make_async_copy(atm_new.at[:, rows, :], atm_out.at[:, rows, :], sems.at[index, 0])
-
-    def ocn_out_of(index):
-        cols = pl.ds(pl.multiple_of(4 * TILE * index, TILE), 4 * TILE)
-        return pltpu.make_async_copy(ocn_new.at[:, :, cols], ocn_out.at[:, :, cols], sems.at[index, 1])
-
-    twos = pairs // 2
+        gain = jnp.concatenate([flux[0][:fields], flux[1][:fields]], axis=0)
+        rows = pl.ds(pl.multiple_of(8 * pair, 8), 8)
+        for level in range(0, levels, 2):
+            here = done[level * fields : level * fields + 8]
+            low = jnp.where(top, here[:, :TILE], turned(here[:, TILE:]))
+            high = jnp.where(top, turned(here[:, :TILE]), here[:, TILE:])
+            atm_new[level, rows, :] = low + atm_w[level : level + 1] * gain
+            atm_new[level + 1, rows, :] = high + atm_w[level + 1 : level + 2] * gain
+
     lead = min(2, twos)
+    for copy in few:
+        copy.wait()
     for index in range(lead):
-        atm_step(index)
-    fill(0, even_op)
+        ocn_step(index)
+    wide_ref[:, :HALO] = edges_ref[0]
+    wide_ref[:, HALO + columns :] = edges_ref[1]
+    fill_pair(even_op, grid_ref, links, metric, 0, first_col, all_cols)
     into(0).wait()
     narrow(0)
     narrow(1)
 
     def two_pairs(index, carry):
         into(index + 1).wait()
-        ocn_step(2 * index, even_op, odd_op, True)
-        ocn_step(2 * index + 1, odd_op, even_op, True)
-        ocn_out_of(index).start()
+        atm_step(2 * index, even_op, odd_op, True)
+        atm_step(2 * index + 1, odd_op, even_op, True)
+        atm_out_of(index).start()
 
         @pl.when(index + lead < twos)
         def _():
-            atm_step(index + lead)
+            ocn_step(index + lead)
 
         return carry
 
     lax.fori_loop(0, twos - 1, two_pairs, 0)
-    ocn_step(pairs - 2, even_op, odd_op, False)
-    ocn_step(pairs - 1, odd_op, None, False)
-    ocn_out_of(twos - 1).start()
+    atm_step(pairs - 2, even_op, odd_op, False)
+    atm_step(pairs - 1, odd_op, None, False)
+    atm_out_of(twos - 1).start()
     for index in range(twos):
         atm_out_of(index).wait()
         ocn_out_of(index).wait()
 
 
-def update(
-    all_cols, atm_wide, ocn_wide, atm_base, ocn_state, edges, ocn_links, ocn_metric, own, other
-):
-    fields, ocn_levels, columns = ocn_state.shape
-    atm_shape = (atm_wide.shape[0], columns // TILE * fields, TILE)
+def update(all_cols, atm_wide, ocn_wide, ocn_base, atm_rows, edges, links, metric, own, other):
+    levels, count, _ = atm_rows.shape
+    ocn_levels, columns = ocn_wide.shape[0], links.shape[1]
+    fields = own.shape[1] // 2
+    ocn_shape = (fields, ocn_levels, columns)
     return pl.pallas_call(
         functools.partial(update_kernel, all_cols),
-        out_shape=(pltpu.HBM(atm_shape, F32), pltpu.HBM(ocn_state.shape, F32)),
-        in_specs=[in_vmem()] * 3 + [in_hbm()] + [in_vmem()] * 5,
+        out_shape=(pltpu.HBM(atm_rows.shape, F32), pltpu.HBM(ocn_shape, F32)),
+        in_specs=[in_hbm()] * 2 + [in_vmem()] + [in_hbm()] * 4 + [in_vmem()] * 2,
         out_specs=(in_hbm(),) * 2,
         scratch_shapes=[
-            pltpu.VMEM((fields * ocn_levels, columns + 2 * HALO), BF16),
+            pltpu.VMEM(atm_wide.shape, F32),
+            pltpu.VMEM(ocn_wide.shape, F32),
+            pltpu.VMEM(edges.shape, BF16),
+            pltpu.VMEM(links.shape, links.dtype),
+            pltpu.VMEM(metric.shape, F32),
+            pltpu.VMEM((fields * levels, columns + 2 * HALO), BF16),
             pltpu.VMEM((2 * (TILE + HALO), 2 * TILE), BF16),
             pltpu.VMEM((2 * (TILE + HALO), 2 * TILE), BF16),
             pltpu.VMEM((TILE + 2 * HALO, TILE), BF16),
-            pltpu.VMEM(ocn_state.shape, F32),
-            pltpu.VMEM(atm_shape, F32),
-            pltpu.VMEM(ocn_state.shape, F32),
+            pltpu.VMEM(atm_rows.shape, F32),
+            pltpu.VMEM(atm_rows.shape, F32),
+            pltpu.VMEM(ocn_shape, F32),
+            pltpu.SemaphoreType.DMA((5,)),
             pltpu.SemaphoreType.DMA((columns // (4 * TILE),)),
             pltpu.SemaphoreType.DMA((columns // (4 * TILE), 2)),
         ],
         compiler_params=limit(20),
         name="update",
-    )(atm_wide, ocn_wide, atm_base, outside(ocn_state), edges, ocn_links, ocn_metric, own, other)
+    )(
+        outside(atm_wide), outside(ocn_wide), ocn_base, outside(atm_rows), outside(edges), outside(links),
+        outside(metric), own, other,
+    )
 
 
 def exchanged(inner, outer, axis):
@@ -617,8 +638,7 @@
     )
     rows = jnp.arange(dev_count * per, dtype=jnp.int32)
     to_slots = (rows[:, None] == goes[None, :]).astype(BF16)
-    to_tiles = (goes[:, None] == rows[None, :]).astype(BF16)
-    return labels, to_slots, to_tiles
+    return labels, to_slots, goes[None, :]
 
 
 def shards(
@@ -646,21 +666,21 @@
         to_rows(atm_state), ocn_state, atm_weights, ocn_weights, paired
     )
     part_other = lax.ppermute(part, "lev", swap)
-    labels, to_slots, to_tiles = routes(tile_source, tile_target, owner_map, blocks, fields, dev_count)
+    labels, to_slots, goes = routes(tile_source, tile_target, owner_map, blocks, fields, dev_count)
     outgoing = contributions(part, part_other, tile_source, tile_weights, to_slots, labels)
     outgoing, inner, outer = lax.optimization_barrier((outgoing, inner, outer))
     arrived = lax.all_to_all(outgoing, BOTH, split_axis=0, concat_axis=0, tiled=True)
     inner, outer = exchanged(inner, outer, "comp")
     xgrid, answer = fluxes(arrived, fields)
-    answer, links = lax.optimization_barrier((answer, atm_links))
+    answer, links = lax.optimization_barrier((answer, ocn_links))
     returned = lax.all_to_all(answer, BOTH, split_axis=0, concat_axis=0, tiled=True)
     all_cols = columns * comp_count
-    atm_base, edges = diffusion(all_cols, paired, to_rows(atm_state), inner, outer, links, atm_metric)
-    returned, atm_base, edges = lax.optimization_barrier((returned, atm_base, edges))
-    spread = spreading(returned, tile_source, tile_weights, to_tiles, blocks, fields)
+    ocn_base, edges = diffusion(all_cols, paired, ocn_state, inner, outer, links, ocn_metric)
+    returned, ocn_base, edges = lax.optimization_barrier((returned, ocn_base, edges))
+    spread = spreading(returned, tile_source, tile_weights, goes, blocks, fields)
     spread_other = lax.ppermute(spread, "lev", swap)
     atm_new, ocn_new = update(
-        all_cols, atm_wide, ocn_wide, atm_base, ocn_state, edges, ocn_links, ocn_metric, spread, spread_other
+        all_cols, atm_wide, ocn_wide, ocn_base, to_rows(atm_state), edges, atm_links, atm_metric, spread, spread_other
     )
     return (from_rows(atm_new, fields), ocn_new, xgrid)
 

time: 44.9 us -> 44.1 us (0.982)
  starting transfers between devices: 17.2 us -> 16.5 us
  Pallas kernels: 19.8 us -> 20.3 us
  waiting for transfers between devices: 5.68 us -> 5.21 us
    all_to_all x1, starting transfers between devices: 4.15 us -> 3.5 us  [shards(): lax.all_to_all(answer, BOTH, split_axis=0, concat_axis=0, tiled=True)]
    pallas_call x1, Pallas kernels: 5.13 us -> 5.67 us  [diffusion(): pl.pallas_call(functools.partial(diffuse_kernel, all_cols, paired), out_s...]
    all_to_all x1, waiting for transfers between devices: 1.57 us -> 1.09 us  [shards(): lax.all_to_all(answer, BOTH, split_axis=0, concat_axis=0, tiled=True)]
  transfers between devices with their start and end apart: 6 -> 6, of which waited for: 4 -> 4; matrix products, arithmetic and copies ran while one was open for 2% -> 2% of each run, Pallas kernels for 14% -> 15%
where the time goes in v3:
time: 44.1 us; the launch traced here: 43.8 us
  Pallas kernels  20.3 us (46%)
  starting transfers between devices  16.5 us (37%)
  waiting for transfers between devices  5.21 us (12%)
  between operations  0.82 us (2%)
  other arithmetic  0.68 us (2%)
    all_to_all x1, starting transfers between devices, shards(): lax.all_to_all(outgoing, BOTH, split_axis=0, concat_axis=0, tiled=True)  7.29 us
    pallas_call x1, Pallas kernels, update(): pl.pallas_call(functools.partial(update_kernel, all_cols), out_shape=(plt...  6.68 us
    pallas_call x1, Pallas kernels, diffusion(): pl.pallas_call(functools.partial(diffuse_kernel, all_cols, paired), out_s...  5.67 us
    all_to_all x1, starting transfers between devices, shards(): lax.all_to_all(answer, BOTH, split_axis=0, concat_axis=0, tiled=True)  3.5 us
    ppermute x1, starting transfers between devices, exchanged(): lax.ppermute(outer, axis, across)  3.27 us
    pallas_call x1, Pallas kernels, surface(): pl.pallas_call(functools.partial(surface_kernel, chunks, paired), out_sha...  2.95 us
    all_to_all x1, waiting for transfers between devices, shards(): lax.all_to_all(outgoing, BOTH, split_axis=0, concat_axis=0, tiled=True)  2.58 us
    pallas_call x1, Pallas kernels, contributions(): pl.pallas_call(functools.partial(contrib_kernel, blocks), out_shape=jax.S...  2.05 us
  transfers between devices with their start and end apart: 6, of which 4 were waited for; matrix products, arithmetic and copies ran while one was open for 2% of the time, Pallas kernels for 15%

profile of v3, /device:TPU:0, one launch (start us, length us, event | category | flops | bytes accessed | tf_op | source)
XLA Modules:
  0.0 43.8 jit_solution(1304285243791693208)
XLA Ops:
  0.6 0.0 copy-start.5
  0.6 0.0 copy-start.6
  0.7 0.0 copy-start.4
  0.7 0.0 copy-start
  0.7 3.0 %surface.1 = (f32[32,8,128]{2,1,0:T(8,128)S(1)}, bf16[304,128]{1,0:T(8,128)(2,1)S(1)}, bf16[304,128]{1,0:T(8,128)(2,1)S(1)}, f32[36,128]{1,0:T(8,128)}, f32[40,128]{1,0:T(8,128)}) custom-call(f32[36,128,128]{2,1,0:T(8,128)} %bitcast.15, f32[4,40,4096]{2,1,0:T(8,128)} %ocn_hbm.3, f32[36]{0:T(128)} %atm_w.1, f32[40]{0:T(128)} %ocn_w.1), custom_call_target="tpu_custom_call" | custom-call | tf_op jit(solution)/shard_map/surface/pallas_call | solution.py:153
  3.6 0.0 copy-start.2
  3.6 0.0 copy-start.3
  3.7 0.5 %collective-permute-start = (f32[32,8,128]{2,1,0:T(8,128)S(1)}, f32[32,8,128]{2,1,0:T(8,128)S(1)}, u32[]{:S(2)}, u32[]{:S(2)}) collective-permute-start(f32[32,8,128]{2,1,0:T(8,128)S(1)} %get-tuple-element.24.own_ref), channel_id=1, source_target_pairs={{0,1},{1,0},{2,3},{3,2},{4,5},{5,4},{6,7},{7,6},{8,9},{9,8},{10,11... | collective-permute-start | bytes 393224 | tf_op jit(solution)/shard_map/ppermute | solution.py:668
  4.2 0.0 copy-done.5
  4.2 0.0 copy-done.6
  4.2 0.2 select_reduce_fusion.1
  4.4 0.0 copy-done.4
  4.4 0.2 convert_reduce_fusion
  4.6 0.1 select_reduce_fusion.2
  4.7 0.1 select_reduce_fusion
  4.8 0.1 convert_element_type.23
  4.9 0.1 fusion.select_ref
  5.0 0.2 collective-permute-done.other_ref
  5.2 0.1 broadcast_in_dim.46.label_ref
  5.2 0.0 copy-done
  5.2 2.0 %contributions.1 = bf16[16,24,128]{2,1,0:T(8,128)(2,1)} custom-call(s32[64]{0:T(128)S(1)} %copy-done.4, f32[32,8,128]{2,1,0:T(8,128)S(1)} %get-tuple-element.24.own_ref, f32[32,8,128]{2,1,0:T(8,128)S(1)} %collective-permute-done.other_ref, bf16[64,128,128]{2,1,0:T(8,128)(2,1)S(1)} %copy-done, bf16[256,512]{1,0:T(8,128)(2,1)S(1)} %fusion.select_ref, ...), custom_call_target="tpu_custom_call" | custom-call | tf_op jit(solution)/shard_map/contributions/pallas_call | solution.py:203
  7.3 7.3 %all-to-all-start = ((bf16[16,24,128]{2,1,0:T(8,128)(2,1)}), bf16[16,24,128]{2,1,0:T(8,128)(2,1)S(1)}, u32[]{:S(2)}, u32[]{:S(2)}) async-start(bf16[16,24,128]{2,1,0:T(8,128)(2,1)} %contributions.1), calls=%async_computation | async-start | bytes 196608 | tf_op jit(solution)/shard_map/all_to_all | solution.py:672
  14.6 1.9 %collective-permute-start.1 = (bf16[304,128]{1,0:T(8,128)(2,1)S(1)}, bf16[304,128]{1,0:T(8,128)(2,1)S(1)}, u32[]{:S(2)}, u32[]{:S(2)}) collective-permute-start(bf16[304,128]{1,0:T(8,128)(2,1)S(1)} %get-tuple-element.30), channel_id=1, source_target_pairs={{0,2},{2,0},{4,6},{6,4},{8,10},{10,8},{12,14},{14,12},{1,3},{3,1},... | collective-permute-start | bytes 233480 | tf_op jit(solution)/shard_map/ppermute | solution.py:614
  16.5 3.3 %collective-permute-start.2 = (bf16[304,128]{1,0:T(8,128)(2,1)S(1)}, bf16[304,128]{1,0:T(8,128)(2,1)S(1)}, u32[]{:S(2)}, u32[]{:S(2)}) collective-permute-start(bf16[304,128]{1,0:T(8,128)(2,1)S(1)} %get-tuple-element.31), channel_id=1, source_target_pairs={{0,14},{2,4},{4,2},{6,8},{8,6},{10,12},{12,10},{14,0},{1,15},{3,5}... | collective-permute-start | bytes 233480 | tf_op jit(solution)/shard_map/ppermute | solution.py:614
  19.8 2.6 %all-to-all-done.arrived_ref = bf16[16,24,128]{2,1,0:T(8,128)(2,1)S(1)} async-done(((bf16[16,24,128]{2,1,0:T(8,128)(2,1)}), bf16[16,24,128]{2,1,0:T(8,128)(2,1)S(1)}, u32[]{:S(2)}, u32[]{:S(2)}) %all-to-all-start) | async-done | bytes 98336 | tf_op jit(solution)/shard_map/all_to_all | solution.py:672
  22.4 1.0 %fluxes.1 = (bf16[16,8,128]{2,1,0:T(8,128)(2,1)}, bf16[16,16,128]{2,1,0:T(8,128)(2,1)}) custom-call(bf16[16,24,128]{2,1,0:T(8,128)(2,1)S(1)} %all-to-all-done.arrived_ref), custom_call_target="tpu_custom_call" | custom-call | tf_op jit(solution)/shard_map/fluxes/pallas_call | solution.py:258
  23.4 3.5 %all-to-all-start.1 = ((bf16[16,16,128]{2,1,0:T(8,128)(2,1)}), bf16[16,16,128]{2,1,0:T(8,128)(2,1)S(1)}, u32[]{:S(2)}, u32[]{:S(2)}) async-start(bf16[16,16,128]{2,1,0:T(8,128)(2,1)} %get-tuple-element.29), calls=%async_computation.1 | async-start | bytes 131072 | tf_op jit(solution)/shard_map/all_to_all | solution.py:676
  27.0 0.0 collective-permute-done.1.inner_ref
  27.0 0.0 collective-permute-done.2.outer_ref
  27.0 0.0 copy-done.2
  27.0 0.0 copy-done.3
  27.0 5.7 %diffusion.1 = (bf16[160,4096]{1,0:T(8,128)(2,1)}, bf16[2,144,128]{2,1,0:T(8,128)(2,1)}) custom-call(f32[4,40,4096]{2,1,0:T(8,128)} %ocn_hbm.3, bf16[304,128]{1,0:T(8,128)(2,1)S(1)} %collective-permute-done.1.inner_ref, bf16[304,128]{1,0:T(8,128)(2,1)S(1)} %collective-permute-done.2.outer_ref, s32[6,4096]{1,0:T(8,128)S(1)} %copy-done.2, f32[6,4096]{1,0:T(8,128)S(1)} %copy-done.3), custom_call_target="tpu_custom_call" | custom-call | tf_op jit(solution)/shard_map/diffusion/pallas_call | solution.py:402
  32.7 0.0 copy-start.1
  32.7 1.1 %all-to-all-done.1.returned_ref = bf16[16,16,128]{2,1,0:T(8,128)(2,1)S(1)} async-done(((bf16[16,16,128]{2,1,0:T(8,128)(2,1)}), bf16[16,16,128]{2,1,0:T(8,128)(2,1)S(1)}, u32[]{:S(2)}, u32[]{:S(2)}) %all-to-all-start.1) | async-done | bytes 65568 | tf_op jit(solution)/shard_map/all_to_all | solution.py:676
  33.8 1.9 %spreading.1.own_ref = f32[32,8,128]{2,1,0:T(8,128)S(1)} custom-call(s32[64]{0:T(128)S(1)} %copy-done.4, bf16[16,16,128]{2,1,0:T(8,128)(2,1)S(1)} %all-to-all-done.1.returned_ref, s32[1,512]{1,0:T(1,128)S(1)} %compare_select_fusion.2.goes_ref, bf16[64,128,128]{2,1,0:T(8,128)(2,1)S(1)} %copy-done), custom_call_target="tpu_custom_call" | custom-call | tf_op jit(solution)/shard_map/spreading/pallas_call | solution.py:446
  35.7 0.0 collective-permute-start.3
  35.8 1.3 %collective-permute-done.3.other_ref = f32[32,8,128]{2,1,0:T(8,128)S(1)} collective-permute-done((f32[32,8,128]{2,1,0:T(8,128)S(1)}, f32[32,8,128]{2,1,0:T(8,128)S(1)}, u32[]{:S(2)}, u32[]{:S(2)}) %collective-permute-start.3) | collective-permute-done | bytes 131104 | tf_op jit(solution)/shard_map/ppermute | solution.py:681
  37.1 0.0 copy-done.1
  37.1 6.7 %update.1 = (f32[36,128,128]{2,1,0:T(8,128)}, f32[4,40,4096]{2,1,0:T(8,128)}) custom-call(f32[36,128]{1,0:T(8,128)} %get-tuple-element.22.atm_w_hbm, f32[40,128]{1,0:T(8,128)} %get-tuple-element.23.ocn_w_hbm, bf16[160,4096]{1,0:T(8,128)(2,1)S(1)} %copy-done.1, f32[36,128,128]{2,1,0:T(8,128)} %bitcast.16, bf16[2,144,128]{2,1,0:T(8,128)(2,1)} %get-tuple-element.36.edges_hbm, ...), custom_call_target="tpu_custom_call" | custom-call | tf_op jit(solution)/shard_map/update/pallas_call | solution.py:577
  (7 shorter events, 0.1 us)
Async XLA Ops:
  0.6 3.6 %copy-start.5 = (s32[256]{0:T(256)S(1)}, s32[256]{0:T(256)}, u32[]{:S(2)}) copy-start(s32[256]{0:T(256)} %param.23) | copy-start | bytes 3076
  0.6 3.5 %copy-start.6 = (s32[64]{0:T(128)S(1)}, s32[64]{0:T(128)}, u32[]{:S(2)}) copy-start(s32[64]{0:T(128)} %param.22) | copy-start | bytes 772
  0.7 3.7 %copy-start.4 = (s32[64]{0:T(128)S(1)}, s32[64]{0:T(128)}, u32[]{:S(2)}) copy-start(s32[64]{0:T(128)} %source_ref.3) | copy-start | bytes 772
  0.7 4.6 %copy-start = (bf16[64,128,128]{2,1,0:T(8,128)(2,1)S(1)}, bf16[64,128,128]{2,1,0:T(8,128)(2,1)}, u32[]{:S(2)}) copy-start(bf16[64,128,128]{2,1,0:T(8,128)(2,1)} %weight_ref.3) | copy-start | bytes 6291460
  3.6 23.3 %copy-start.2 = (s32[6,4096]{1,0:T(8,128)S(1)}, s32[6,4096]{1,0:T(8,128)}, u32[]{:S(2)}) copy-start(s32[6,4096]{1,0:T(8,128)} %links) | copy-start | bytes 294916
  3.6 23.3 %copy-start.3 = (f32[6,4096]{1,0:T(8,128)S(1)}, f32[6,4096]{1,0:T(8,128)}, u32[]{:S(2)}) copy-start(f32[6,4096]{1,0:T(8,128)} %metric.1) | copy-start | bytes 294916
  3.7 1.5 %collective-permute-start = (f32[32,8,128]{2,1,0:T(8,128)S(1)}, f32[32,8,128]{2,1,0:T(8,128)S(1)}, u32[]{:S(2)}, u32[]{:S(2)}) collective-permute-start(f32[32,8,128]{2,1,0:T(8,128)S(1)} %get-tuple-element.24.own_ref), channel_id=1, source_target_pairs={{0,1},{1,0},{2,3},{3,2},{4,5},{5,4},{6,7},{7,6},{8,9},{9,8},{10,11... | collective-permute-start | bytes 393224 | tf_op jit(solution)/shard_map/ppermute | solution.py:668
  7.3 15.1 %all-to-all-start = ((bf16[16,24,128]{2,1,0:T(8,128)(2,1)}), bf16[16,24,128]{2,1,0:T(8,128)(2,1)S(1)}, u32[]{:S(2)}, u32[]{:S(2)}) async-start(bf16[16,24,128]{2,1,0:T(8,128)(2,1)} %contributions.1), calls=%async_computation | async-start | bytes 196608 | tf_op jit(solution)/shard_map/all_to_all | solution.py:672
  14.6 12.4 %collective-permute-start.1 = (bf16[304,128]{1,0:T(8,128)(2,1)S(1)}, bf16[304,128]{1,0:T(8,128)(2,1)S(1)}, u32[]{:S(2)}, u32[]{:S(2)}) collective-permute-start(bf16[304,128]{1,0:T(8,128)(2,1)S(1)} %get-tuple-element.30), channel_id=1, source_target_pairs={{0,2},{2,0},{4,6},{6,4},{8,10},{10,8},{12,14},{14,12},{1,3},{3,1},... | collective-permute-start | bytes 233480 | tf_op jit(solution)/shard_map/ppermute | solution.py:614
  16.5 10.4 %collective-permute-start.2 = (bf16[304,128]{1,0:T(8,128)(2,1)S(1)}, bf16[304,128]{1,0:T(8,128)(2,1)S(1)}, u32[]{:S(2)}, u32[]{:S(2)}) collective-permute-start(bf16[304,128]{1,0:T(8,128)(2,1)S(1)} %get-tuple-element.31), channel_id=1, source_target_pairs={{0,14},{2,4},{4,2},{6,8},{8,6},{10,12},{12,10},{14,0},{1,15},{3,5}... | collective-permute-start | bytes 233480 | tf_op jit(solution)/shard_map/ppermute | solution.py:614
  23.4 10.4 %all-to-all-start.1 = ((bf16[16,16,128]{2,1,0:T(8,128)(2,1)}), bf16[16,16,128]{2,1,0:T(8,128)(2,1)S(1)}, u32[]{:S(2)}, u32[]{:S(2)}) async-start(bf16[16,16,128]{2,1,0:T(8,128)(2,1)} %get-tuple-element.29), calls=%async_computation.1 | async-start | bytes 131072 | tf_op jit(solution)/shard_map/all_to_all | solution.py:676
  32.7 4.4 %copy-start.1 = (bf16[160,4096]{1,0:T(8,128)(2,1)S(1)}, bf16[160,4096]{1,0:T(8,128)(2,1)}, u32[]{:S(2)}) copy-start(bf16[160,4096]{1,0:T(8,128)(2,1)} %get-tuple-element.35.ocn_base) | copy-start | bytes 3932164
  35.7 1.4 %collective-permute-start.3 = (f32[32,8,128]{2,1,0:T(8,128)S(1)}, f32[32,8,128]{2,1,0:T(8,128)S(1)}, u32[]{:S(2)}, u32[]{:S(2)}) collective-permute-start(f32[32,8,128]{2,1,0:T(8,128)S(1)} %spreading.1.own_ref), channel_id=1, source_target_pairs={{0,1},{1,0},{2,3},{3,2},{4,5},{5,4},{6,7},{7,6},{8,9},{9,8},{10,11... | collective-permute-start | bytes 393224 | tf_op jit(solution)/shard_map/ppermute | solution.py:681

commit v4 on v3

--- a/solution.py
+++ b/solution.py
@@ -149,7 +149,7 @@
     levels, count, _ = atm_rows.shape
     fields, ocn_levels, columns = ocn_state.shape
     rows = fields * (levels + ocn_levels)
-    chunks = 4
+    chunks = 8
     return pl.pallas_call(
         functools.partial(surface_kernel, chunks, paired),
         out_shape=(
@@ -537,10 +537,12 @@
             atm_new[level + 1, rows, :] = high + atm_w[level + 1 : level + 2] * gain
 
     lead = min(2, twos)
-    for copy in few:
+    for copy in few[:2]:
         copy.wait()
     for index in range(lead):
         ocn_step(index)
+    for copy in few[2:]:
+        copy.wait()
     wide_ref[:, :HALO] = edges_ref[0]
     wide_ref[:, HALO + columns :] = edges_ref[1]
     fill_pair(even_op, grid_ref, links, metric, 0, first_col, all_cols)

time: 44.1 us -> 44 us (level)
  no operation moved by 1% of the time
where the time goes in v4:
time: 44 us; the launch traced here: 43.7 us
  Pallas kernels  20.2 us (46%)
  starting transfers between devices  16.5 us (38%)
  waiting for transfers between devices  5.21 us (12%)
  between operations  0.82 us (2%)
  other arithmetic  0.68 us (2%)
    all_to_all x1, starting transfers between devices, shards(): lax.all_to_all(outgoing, BOTH, split_axis=0, concat_axis=0, tiled=True)  7.3 us
    pallas_call x1, Pallas kernels, update(): pl.pallas_call(functools.partial(update_kernel, all_cols), out_shape=(plt...  6.6 us
    pallas_call x1, Pallas kernels, diffusion(): pl.pallas_call(functools.partial(diffuse_kernel, all_cols, paired), out_s...  5.67 us
    all_to_all x1, starting transfers between devices, shards(): lax.all_to_all(answer, BOTH, split_axis=0, concat_axis=0, tiled=True)  3.5 us
    ppermute x1, starting transfers between devices, exchanged(): lax.ppermute(outer, axis, across)  3.27 us
    pallas_call x1, Pallas kernels, surface(): pl.pallas_call(functools.partial(surface_kernel, chunks, paired), out_sha...  2.91 us
    all_to_all x1, waiting for transfers between devices, shards(): lax.all_to_all(outgoing, BOTH, split_axis=0, concat_axis=0, tiled=True)  2.58 us
    pallas_call x1, Pallas kernels, contributions(): pl.pallas_call(functools.partial(contrib_kernel, blocks), out_shape=jax.S...  2.04 us
  transfers between devices with their start and end apart: 6, of which 4 were waited for; matrix products, arithmetic and copies ran while one was open for 2% of the time, Pallas kernels for 15%

profile of v4, /device:TPU:0, one launch (start us, length us, event | category | flops | bytes accessed | tf_op | source)
XLA Modules:
  0.0 43.7 jit_solution(4914192150644936181)
XLA Ops:
  0.6 0.0 copy-start.5
  0.6 0.0 copy-start.6
  0.7 0.0 copy-start.4
  0.7 0.0 copy-start
  0.7 2.9 %surface.1 = (f32[32,8,128]{2,1,0:T(8,128)S(1)}, bf16[304,128]{1,0:T(8,128)(2,1)S(1)}, bf16[304,128]{1,0:T(8,128)(2,1)S(1)}, f32[36,128]{1,0:T(8,128)}, f32[40,128]{1,0:T(8,128)}) custom-call(f32[36,128,128]{2,1,0:T(8,128)} %bitcast.15, f32[4,40,4096]{2,1,0:T(8,128)} %ocn_hbm.3, f32[36]{0:T(128)} %atm_w.1, f32[40]{0:T(128)} %ocn_w.1), custom_call_target="tpu_custom_call" | custom-call | tf_op jit(solution)/shard_map/surface/pallas_call | solution.py:153
  3.6 0.0 copy-start.2
  3.6 0.0 copy-start.3
  3.6 0.5 %collective-permute-start = (f32[32,8,128]{2,1,0:T(8,128)S(1)}, f32[32,8,128]{2,1,0:T(8,128)S(1)}, u32[]{:S(2)}, u32[]{:S(2)}) collective-permute-start(f32[32,8,128]{2,1,0:T(8,128)S(1)} %get-tuple-element.24.own_ref), channel_id=1, source_target_pairs={{0,1},{1,0},{2,3},{3,2},{4,5},{5,4},{6,7},{7,6},{8,9},{9,8},{10,11... | collective-permute-start | bytes 393224 | tf_op jit(solution)/shard_map/ppermute | solution.py:670
  4.1 0.0 copy-done.5
  4.1 0.0 copy-done.6
  4.1 0.2 select_reduce_fusion.1
  4.3 0.0 copy-done.4
  4.4 0.2 convert_reduce_fusion
  4.5 0.1 select_reduce_fusion.2
  4.7 0.1 select_reduce_fusion
  4.8 0.1 convert_element_type.23
  4.9 0.1 fusion.select_ref
  4.9 0.2 collective-permute-done.other_ref
  5.1 0.1 broadcast_in_dim.46.label_ref
  5.2 0.0 copy-done
  5.2 2.0 %contributions.1 = bf16[16,24,128]{2,1,0:T(8,128)(2,1)} custom-call(s32[64]{0:T(128)S(1)} %copy-done.4, f32[32,8,128]{2,1,0:T(8,128)S(1)} %get-tuple-element.24.own_ref, f32[32,8,128]{2,1,0:T(8,128)S(1)} %collective-permute-done.other_ref, bf16[64,128,128]{2,1,0:T(8,128)(2,1)S(1)} %copy-done, bf16[256,512]{1,0:T(8,128)(2,1)S(1)} %fusion.select_ref, ...), custom_call_target="tpu_custom_call" | custom-call | tf_op jit(solution)/shard_map/contributions/pallas_call | solution.py:203
  7.3 7.3 %all-to-all-start = ((bf16[16,24,128]{2,1,0:T(8,128)(2,1)}), bf16[16,24,128]{2,1,0:T(8,128)(2,1)S(1)}, u32[]{:S(2)}, u32[]{:S(2)}) async-start(bf16[16,24,128]{2,1,0:T(8,128)(2,1)} %contributions.1), calls=%async_computation | async-start | bytes 196608 | tf_op jit(solution)/shard_map/all_to_all | solution.py:674
  14.6 1.9 %collective-permute-start.1 = (bf16[304,128]{1,0:T(8,128)(2,1)S(1)}, bf16[304,128]{1,0:T(8,128)(2,1)S(1)}, u32[]{:S(2)}, u32[]{:S(2)}) collective-permute-start(bf16[304,128]{1,0:T(8,128)(2,1)S(1)} %get-tuple-element.30), channel_id=1, source_target_pairs={{0,2},{2,0},{4,6},{6,4},{8,10},{10,8},{12,14},{14,12},{1,3},{3,1},... | collective-permute-start | bytes 233480 | tf_op jit(solution)/shard_map/ppermute | solution.py:616
  16.5 3.3 %collective-permute-start.2 = (bf16[304,128]{1,0:T(8,128)(2,1)S(1)}, bf16[304,128]{1,0:T(8,128)(2,1)S(1)}, u32[]{:S(2)}, u32[]{:S(2)}) collective-permute-start(bf16[304,128]{1,0:T(8,128)(2,1)S(1)} %get-tuple-element.31), channel_id=1, source_target_pairs={{0,14},{2,4},{4,2},{6,8},{8,6},{10,12},{12,10},{14,0},{1,15},{3,5}... | collective-permute-start | bytes 233480 | tf_op jit(solution)/shard_map/ppermute | solution.py:616
  19.7 2.6 %all-to-all-done.arrived_ref = bf16[16,24,128]{2,1,0:T(8,128)(2,1)S(1)} async-done(((bf16[16,24,128]{2,1,0:T(8,128)(2,1)}), bf16[16,24,128]{2,1,0:T(8,128)(2,1)S(1)}, u32[]{:S(2)}, u32[]{:S(2)}) %all-to-all-start) | async-done | bytes 98336 | tf_op jit(solution)/shard_map/all_to_all | solution.py:674
  22.3 1.0 %fluxes.1 = (bf16[16,8,128]{2,1,0:T(8,128)(2,1)}, bf16[16,16,128]{2,1,0:T(8,128)(2,1)}) custom-call(bf16[16,24,128]{2,1,0:T(8,128)(2,1)S(1)} %all-to-all-done.arrived_ref), custom_call_target="tpu_custom_call" | custom-call | tf_op jit(solution)/shard_map/fluxes/pallas_call | solution.py:258
  23.4 3.5 %all-to-all-start.1 = ((bf16[16,16,128]{2,1,0:T(8,128)(2,1)}), bf16[16,16,128]{2,1,0:T(8,128)(2,1)S(1)}, u32[]{:S(2)}, u32[]{:S(2)}) async-start(bf16[16,16,128]{2,1,0:T(8,128)(2,1)} %get-tuple-element.29), calls=%async_computation.1 | async-start | bytes 131072 | tf_op jit(solution)/shard_map/all_to_all | solution.py:678
  26.9 0.0 collective-permute-done.1.inner_ref
  26.9 0.0 collective-permute-done.2.outer_ref
  26.9 0.0 copy-done.2
  26.9 0.0 copy-done.3
  27.0 5.7 %diffusion.1 = (bf16[160,4096]{1,0:T(8,128)(2,1)}, bf16[2,144,128]{2,1,0:T(8,128)(2,1)}) custom-call(f32[4,40,4096]{2,1,0:T(8,128)} %ocn_hbm.3, bf16[304,128]{1,0:T(8,128)(2,1)S(1)} %collective-permute-done.1.inner_ref, bf16[304,128]{1,0:T(8,128)(2,1)S(1)} %collective-permute-done.2.outer_ref, s32[6,4096]{1,0:T(8,128)S(1)} %copy-done.2, f32[6,4096]{1,0:T(8,128)S(1)} %copy-done.3), custom_call_target="tpu_custom_call" | custom-call | tf_op jit(solution)/shard_map/diffusion/pallas_call | solution.py:402
  32.6 0.0 copy-start.1
  32.6 1.1 %all-to-all-done.1.returned_ref = bf16[16,16,128]{2,1,0:T(8,128)(2,1)S(1)} async-done(((bf16[16,16,128]{2,1,0:T(8,128)(2,1)}), bf16[16,16,128]{2,1,0:T(8,128)(2,1)S(1)}, u32[]{:S(2)}, u32[]{:S(2)}) %all-to-all-start.1) | async-done | bytes 65568 | tf_op jit(solution)/shard_map/all_to_all | solution.py:678
  33.7 1.9 %spreading.1.own_ref = f32[32,8,128]{2,1,0:T(8,128)S(1)} custom-call(s32[64]{0:T(128)S(1)} %copy-done.4, bf16[16,16,128]{2,1,0:T(8,128)(2,1)S(1)} %all-to-all-done.1.returned_ref, s32[1,512]{1,0:T(1,128)S(1)} %compare_select_fusion.2.goes_ref, bf16[64,128,128]{2,1,0:T(8,128)(2,1)S(1)} %copy-done), custom_call_target="tpu_custom_call" | custom-call | tf_op jit(solution)/shard_map/spreading/pallas_call | solution.py:446
  35.7 0.0 collective-permute-start.3
  35.7 1.3 %collective-permute-done.3.other_ref = f32[32,8,128]{2,1,0:T(8,128)S(1)} collective-permute-done((f32[32,8,128]{2,1,0:T(8,128)S(1)}, f32[32,8,128]{2,1,0:T(8,128)S(1)}, u32[]{:S(2)}, u32[]{:S(2)}) %collective-permute-start.3) | collective-permute-done | bytes 131104 | tf_op jit(solution)/shard_map/ppermute | solution.py:683
  37.1 0.0 copy-done.1
  37.1 6.6 %update.1 = (f32[36,128,128]{2,1,0:T(8,128)}, f32[4,40,4096]{2,1,0:T(8,128)}) custom-call(f32[36,128]{1,0:T(8,128)} %get-tuple-element.22.atm_w_hbm, f32[40,128]{1,0:T(8,128)} %get-tuple-element.23.ocn_w_hbm, bf16[160,4096]{1,0:T(8,128)(2,1)S(1)} %copy-done.1, f32[36,128,128]{2,1,0:T(8,128)} %bitcast.16, bf16[2,144,128]{2,1,0:T(8,128)(2,1)} %get-tuple-element.36.edges_hbm, ...), custom_call_target="tpu_custom_call" | custom-call | tf_op jit(solution)/shard_map/update/pallas_call | solution.py:579
  (7 shorter events, 0.1 us)
Async XLA Ops:
  0.6 3.5 %copy-start.5 = (s32[256]{0:T(256)S(1)}, s32[256]{0:T(256)}, u32[]{:S(2)}) copy-start(s32[256]{0:T(256)} %param.23) | copy-start | bytes 3076
  0.6 3.5 %copy-start.6 = (s32[64]{0:T(128)S(1)}, s32[64]{0:T(128)}, u32[]{:S(2)}) copy-start(s32[64]{0:T(128)} %param.22) | copy-start | bytes 772
  0.7 3.7 %copy-start.4 = (s32[64]{0:T(128)S(1)}, s32[64]{0:T(128)}, u32[]{:S(2)}) copy-start(s32[64]{0:T(128)} %source_ref.3) | copy-start | bytes 772
  0.7 4.5 %copy-start = (bf16[64,128,128]{2,1,0:T(8,128)(2,1)S(1)}, bf16[64,128,128]{2,1,0:T(8,128)(2,1)}, u32[]{:S(2)}) copy-start(bf16[64,128,128]{2,1,0:T(8,128)(2,1)} %weight_ref.3) | copy-start | bytes 6291460
  3.6 23.3 %copy-start.2 = (s32[6,4096]{1,0:T(8,128)S(1)}, s32[6,4096]{1,0:T(8,128)}, u32[]{:S(2)}) copy-start(s32[6,4096]{1,0:T(8,128)} %links) | copy-start | bytes 294916
  3.6 23.3 %copy-start.3 = (f32[6,4096]{1,0:T(8,128)S(1)}, f32[6,4096]{1,0:T(8,128)}, u32[]{:S(2)}) copy-start(f32[6,4096]{1,0:T(8,128)} %metric.1) | copy-start | bytes 294916
  3.6 1.5 %collective-permute-start = (f32[32,8,128]{2,1,0:T(8,128)S(1)}, f32[32,8,128]{2,1,0:T(8,128)S(1)}, u32[]{:S(2)}, u32[]{:S(2)}) collective-permute-start(f32[32,8,128]{2,1,0:T(8,128)S(1)} %get-tuple-element.24.own_ref), channel_id=1, source_target_pairs={{0,1},{1,0},{2,3},{3,2},{4,5},{5,4},{6,7},{7,6},{8,9},{9,8},{10,11... | collective-permute-start | bytes 393224 | tf_op jit(solution)/shard_map/ppermute | solution.py:670
  7.3 15.1 %all-to-all-start = ((bf16[16,24,128]{2,1,0:T(8,128)(2,1)}), bf16[16,24,128]{2,1,0:T(8,128)(2,1)S(1)}, u32[]{:S(2)}, u32[]{:S(2)}) async-start(bf16[16,24,128]{2,1,0:T(8,128)(2,1)} %contributions.1), calls=%async_computation | async-start | bytes 196608 | tf_op jit(solution)/shard_map/all_to_all | solution.py:674
  14.6 12.4 %collective-permute-start.1 = (bf16[304,128]{1,0:T(8,128)(2,1)S(1)}, bf16[304,128]{1,0:T(8,128)(2,1)S(1)}, u32[]{:S(2)}, u32[]{:S(2)}) collective-permute-start(bf16[304,128]{1,0:T(8,128)(2,1)S(1)} %get-tuple-element.30), channel_id=1, source_target_pairs={{0,2},{2,0},{4,6},{6,4},{8,10},{10,8},{12,14},{14,12},{1,3},{3,1},... | collective-permute-start | bytes 233480 | tf_op jit(solution)/shard_map/ppermute | solution.py:616
  16.5 10.4 %collective-permute-start.2 = (bf16[304,128]{1,0:T(8,128)(2,1)S(1)}, bf16[304,128]{1,0:T(8,128)(2,1)S(1)}, u32[]{:S(2)}, u32[]{:S(2)}) collective-permute-start(bf16[304,128]{1,0:T(8,128)(2,1)S(1)} %get-tuple-element.31), channel_id=1, source_target_pairs={{0,14},{2,4},{4,2},{6,8},{8,6},{10,12},{12,10},{14,0},{1,15},{3,5}... | collective-permute-start | bytes 233480 | tf_op jit(solution)/shard_map/ppermute | solution.py:616
  23.4 10.4 %all-to-all-start.1 = ((bf16[16,16,128]{2,1,0:T(8,128)(2,1)}), bf16[16,16,128]{2,1,0:T(8,128)(2,1)S(1)}, u32[]{:S(2)}, u32[]{:S(2)}) async-start(bf16[16,16,128]{2,1,0:T(8,128)(2,1)} %get-tuple-element.29), calls=%async_computation.1 | async-start | bytes 131072 | tf_op jit(solution)/shard_map/all_to_all | solution.py:678
  32.6 4.4 %copy-start.1 = (bf16[160,4096]{1,0:T(8,128)(2,1)S(1)}, bf16[160,4096]{1,0:T(8,128)(2,1)}, u32[]{:S(2)}) copy-start(bf16[160,4096]{1,0:T(8,128)(2,1)} %get-tuple-element.35.ocn_base) | copy-start | bytes 3932164
  35.7 1.4 %collective-permute-start.3 = (f32[32,8,128]{2,1,0:T(8,128)S(1)}, f32[32,8,128]{2,1,0:T(8,128)S(1)}, u32[]{:S(2)}, u32[]{:S(2)}) collective-permute-start(f32[32,8,128]{2,1,0:T(8,128)S(1)} %spreading.1.own_ref), channel_id=1, source_target_pairs={{0,1},{1,0},{2,3},{3,2},{4,5},{5,4},{6,7},{7,6},{8,9},{9,8},{10,11... | collective-permute-start | bytes 393224 | tf_op jit(solution)/shard_map/ppermute | solution.py:683
